TPU v7x, 32 devices: a whole 2x2x4 slice. The times are simulated.
32 devices in a mesh: groups: 1, row: 16 (over z, y, core), chan: 2 (over x), sub: 1.
Axes of the slice: x: 2, y: 2, z: 4, core: 2. Of those that a mesh axis runs over, the one named last changes fastest.
Arguments:
- pair_act: bfloat16 [256, 256, 128], P(('groups', 'row'), 'sub'), may hold values from -6 to 6
- residue_valid: int32 [256], P('groups'), may hold values 0 or 1
- in_gain: float32 [128], replicated, may hold values from 0.1 to 1.9
- w_left: bfloat16 [128, 128], P(None, 'chan'), may hold values from -0.5 to 0.5
- w_left_gate: bfloat16 [128, 128], P(None, 'chan'), may hold values from -0.5 to 0.5
- w_right: bfloat16 [128, 128], P(None, 'chan'), may hold values from -0.5 to 0.5
- w_right_gate: bfloat16 [128, 128], P(None, 'chan'), may hold values from -0.5 to 0.5
- out_gain: float32 [128], replicated, may hold values from 0.1 to 1.9
- w_out: bfloat16 [128, 128], replicated, may hold values from -0.5 to 0.5
- w_out_gate: bfloat16 [128, 128], replicated, may hold values from -0.5 to 0.5
Outputs:
- update: bfloat16 [256, 256, 128], P(('groups', 'row'), 'sub')
All inputs are finite; a program needn't handle non-finite values.
Results may differ from a plain program's by a relative error of at most 0.017.
Values may be sent and summed in bfloat16 or wider, within the bound.
A program may use at most 64 MiB of HBM per device.

v0:
```python
import jax
import jax.numpy as jnp
from jax import lax
from jax.sharding import PartitionSpec as P


def norm_axis(values, gain, axis):
    mean = jnp.mean(values, axis=axis, keepdims=True)
    centered = values - mean
    variance = jnp.mean(centered * centered, axis=axis, keepdims=True)
    return centered * lax.rsqrt(variance + 1e-05) * gain


def finish_block(tri_block, normed_block, out_gain, w_out, w_out_gate):
    tri_norm = norm_axis(tri_block.astype(jnp.float32), out_gain[:, None, None], 0).astype(
        jnp.bfloat16
    )
    projected = jnp.einsum("hij,hc->ijc", tri_norm, w_out, preferred_element_type=jnp.float32)
    gating = jnp.einsum("ijc,cd->ijd", normed_block, w_out_gate, preferred_element_type=jnp.float32)
    return (jax.nn.sigmoid(gating) * projected).astype(jnp.bfloat16)


def body(
    pair_act,
    residue_valid,
    in_gain,
    w_left,
    w_left_gate,
    w_right,
    w_right_gate,
    out_gain,
    w_out,
    w_out_gate,
):
    row_count = pair_act.shape[0]
    col_count = pair_act.shape[1]
    row_first = lax.axis_index("row") * row_count
    col_first = lax.axis_index("sub") * col_count
    normed = norm_axis(pair_act.astype(jnp.float32), in_gain, 2).astype(jnp.bfloat16)
    valid = residue_valid.astype(jnp.float32)
    row_valid = lax.dynamic_slice_in_dim(valid, row_first, row_count)
    col_valid = lax.dynamic_slice_in_dim(valid, col_first, col_count)
    weight = (row_valid[:, None] * col_valid[None, :])[None, :, :]

    def project(w_lin, w_gate):
        linear = jnp.einsum("ikc,ch->hik", normed, w_lin, preferred_element_type=jnp.float32)
        gating = jnp.einsum("ikc,ch->hik", normed, w_gate, preferred_element_type=jnp.float32)
        return (jax.nn.sigmoid(gating) * linear * weight).astype(jnp.bfloat16)

    left = project(w_left, w_left_gate)
    right = project(w_right, w_right_gate)
    right_all = lax.all_gather(right, "row", axis=1, tiled=True)
    partial_tri = lax.dot_general(
        left, right_all, (((2,), (2,)), ((0,), (0,))), preferred_element_type=jnp.float32
    )
    tri_half = lax.psum_scatter(
        partial_tri.astype(jnp.bfloat16), "sub", scatter_dimension=2, tiled=True
    )
    tri_full = lax.all_gather(tri_half, "chan", axis=0, tiled=True)
    update = finish_block(tri_full, normed, out_gain, w_out, w_out_gate)
    return update


def solution(mesh):
    placed = (
        P(("groups", "row"), "sub", None),
        P("groups"),
        P(),
        P(None, "chan"),
        P(None, "chan"),
        P(None, "chan"),
        P(None, "chan"),
        P(),
        P(),
        P(),
    )
    return jax.shard_map(
        body,
        mesh=mesh,
        in_specs=placed,
        out_specs=P(("groups", "row"), "sub", None),
        check_vma=False,
    )
```

profile of v0, /device:TPU:0, one launch (start us, length us, event | category | flops | bytes accessed | tf_op | source)
XLA Modules:
  0.0 137.8 jit_solution(12169519718571291257)
XLA Ops:
  6.5 0.0 copy-start
  6.5 0.0 all-gather.3.cloned.1.call-start
  6.6 0.0 copy-start.8
  6.6 1.7 %convert_reduce_fusion.1 = f32[16,256]{1,0:T(8,128)S(1)} fusion(bf16[16,256,128]{2,1,0:T(8,128)(2,1)} %param.10), kind=kLoop, calls=%fused_computation.3 | loop fusion | flops 1044480 | bytes 1064960 | tf_op jit(solution)/shard_map/reduce_sum | solution.py:8
  8.3 2.3 %fusion.7 = f32[16,256]{1,0:T(8,128)S(1)} fusion(bf16[16,256,128]{2,1,0:T(8,128)(2,1)} %param.10, f32[16,256]{1,0:T(8,128)S(1)} %broadcast_multiply_fusion.2), kind=kLoop, calls=%fused_computation.11 | loop fusion | flops 2093056 | bytes 1081344 | tf_op jit(solution)/shard_map/reduce_sum | solution.py:10
  10.6 0.0 copy-done.2
  10.6 0.0 copy-done.5
  10.7 0.0 copy-start.3
  10.7 2.8 %fusion.28 = f32[16,256,64]{1,2,0:T(8,128)S(1)} fusion(bf16[128,64]{0,1:T(8,128)(2,1)S(1)} %copy-done.7, bf16[16,256,128]{2,1,0:T(8,128)(2,1)S(1)} %copy-done.2, f32[128]{0:T(128)S(1)} %copy-done.5, f32[16,256]{1,0:T(8,128)S(1)} %add_rsqrt_fusion.1, f32[16,256]{1,0:T(8,128)S(1)} %broadcast_multiply_fusion.2), kind=kOutput, calls=%fused_computation.37 | convolution fusion | flops 69730304 | bytes 2146816 | tf_op jit(solution)/shard_map/ikc,ch->hik/dot_general | solution.py:46
  13.5 2.8 %fusion.30 = f32[16,256,64]{1,2,0:T(8,128)S(1)} fusion(bf16[128,64]{0,1:T(8,128)(2,1)S(1)} %copy-done.8, bf16[16,256,128]{2,1,0:T(8,128)(2,1)S(1)} %copy-done.2, f32[128]{0:T(128)S(1)} %copy-done.5, f32[16,256]{1,0:T(8,128)S(1)} %add_rsqrt_fusion.1, f32[16,256]{1,0:T(8,128)S(1)} %broadcast_multiply_fusion.2), kind=kOutput, calls=%fused_computation.39 | convolution fusion | flops 69730304 | bytes 2146816 | tf_op jit(solution)/shard_map/ikc,ch->hik/dot_general | solution.py:47
  16.3 0.0 copy-start.9
  16.3 0.1 dynamic_slice.4
  16.4 0.1 broadcast_multiply_fusion
  16.5 2.0 %fusion.24 = bf16[64,16,256]{2,1,0:T(8,128)(2,1)} fusion(f32[16,256]{1,0:T(8,128)S(1)} %broadcast_multiply_fusion, f32[16,256,64]{1,2,0:T(8,128)S(1)} %fusion.28, f32[16,256,64]{1,2,0:T(8,128)S(1)} %fusion.30), kind=kLoop, calls=%fused_computation.33 | loop fusion | flops 1572864 | bytes 2637824 | tf_op jit(solution)/shard_map/convert_element_type | solution.py:48
  18.4 0.0 all-gather.3.cloned.1.call-update
  18.5 0.0 all-gather.5.cloned.1.call-start
  18.5 0.0 copy-done.9
  18.5 2.8 %fusion.32 = f32[16,256,64]{1,2,0:T(8,128)S(1)} fusion(bf16[128,64]{0,1:T(8,128)(2,1)S(1)} %copy-done.9, bf16[16,256,128]{2,1,0:T(8,128)(2,1)S(1)} %copy-done.2, f32[128]{0:T(128)S(1)} %copy-done.5, f32[16,256]{1,0:T(8,128)S(1)} %add_rsqrt_fusion.1, f32[16,256]{1,0:T(8,128)S(1)} %broadcast_multiply_fusion.2), kind=kOutput, calls=%fused_computation.41 | convolution fusion | flops 69730304 | bytes 2146816 | tf_op jit(solution)/shard_map/ikc,ch->hik/dot_general | solution.py:46
  21.3 2.8 %fusion.34 = f32[16,256,64]{1,2,0:T(8,128)S(1)} fusion(bf16[128,64]{0,1:T(8,128)(2,1)S(1)} %copy-done.10, bf16[16,256,128]{2,1,0:T(8,128)(2,1)S(1)} %copy-done.2, f32[128]{0:T(128)S(1)} %copy-done.5, f32[16,256]{1,0:T(8,128)S(1)} %add_rsqrt_fusion.1, f32[16,256]{1,0:T(8,128)S(1)} %broadcast_multiply_fusion.2), kind=kOutput, calls=%fused_computation.43 | convolution fusion | flops 69730304 | bytes 2146816 | tf_op jit(solution)/shard_map/ikc,ch->hik/dot_general | solution.py:47
  24.1 75.3 %all-gather.3.cloned.1.call-done = bf16[64,256,256]{2,1,0:T(8,128)(2,1)} async-done(((bf16[64,16,256]{2,1,0:T(8,128)(2,1)}), bf16[64,256,256]{2,1,0:T(8,128)(2,1)}) %all-gather.3.cloned.1.call-update) | async-done | bytes 8388624 | tf_op jit(solution)/shard_map/all_gather | solution.py:52
  99.4 6.5 %convolution_convert_fusion = bf16[64,16,256]{2,1,0:T(8,128)(2,1)} fusion(bf16[64,256,256]{2,1,0:T(8,128)(2,1)} %all-gather.3.cloned.1.call-done, f32[16,256,64]{1,2,0:T(8,128)S(1)} %fusion.32, f32[16,256,64]{1,2,0:T(8,128)S(1)} %fusion.34, f32[16,256]{1,0:T(8,128)S(1)} %broadcast_multiply_fusion), kind=kOutput, calls=%fused_computation.15 | convolution fusion | flops 136052736 | bytes 11026432 | tf_op jit(solution)/shard_map/dot_general | solution.py:53
  105.9 0.0 all-gather.5.cloned.1.call-update
  105.9 0.0 copy-done
  106.0 0.0 copy-start.4
  106.0 1.5 %fusion.26 = f32[16,256,128]{2,1,0:T(8,128)S(1)} fusion(bf16[128,128]{1,0:T(8,128)(2,1)S(1)} %copy-done, bf16[16,256,128]{2,1,0:T(8,128)(2,1)S(1)} %copy-done.2, f32[128]{0:T(128)S(1)} %copy-done.5, f32[16,256]{1,0:T(8,128)S(1)} %add_rsqrt_fusion.1, f32[16,256]{1,0:T(8,128)S(1)} %broadcast_multiply_fusion.2), kind=kOutput, calls=%fused_computation.35 | convolution fusion | flops 136839168 | bytes 3211776 | tf_op jit(solution)/shard_map/ijc,cd->ijd/dot_general | solution.py:19
  107.5 0.0 copy-start.6
  107.5 18.1 %all-gather.5.cloned.1.call-done = bf16[128,16,256]{2,1,0:T(8,128)(2,1)} async-done(((bf16[64,16,256]{2,1,0:T(8,128)(2,1)}), bf16[128,16,256]{2,1,0:T(8,128)(2,1)}) %all-gather.5.cloned.1.call-update) | async-done | bytes 1048592 | tf_op jit(solution)/shard_map/all_gather | solution.py:59
  125.6 1.5 %convert_reduce_fusion = f32[16,256]{1,0:T(8,128)S(1)} fusion(bf16[128,16,256]{2,1,0:T(8,128)(2,1)} %all-gather.5.cloned.1.call-done), kind=kLoop, calls=%fused_computation.1 | loop fusion | flops 1044480 | bytes 1064960 | tf_op jit(solution)/shard_map/reduce_sum | solution.py:8
  127.1 1.6 %fusion.4 = f32[16,256]{1,0:T(8,128)S(1)} fusion(bf16[128,16,256]{2,1,0:T(8,128)(2,1)} %all-gather.5.cloned.1.call-done, f32[16,256]{1,0:T(8,128)S(1)} %broadcast_multiply_fusion.1), kind=kLoop, calls=%fused_computation.8 | loop fusion | flops 2093056 | bytes 1081344 | tf_op jit(solution)/shard_map/reduce_sum | solution.py:10
  128.7 0.0 copy-done.1
  128.7 0.3 fusion.6
  129.0 1.9 %multiply_convert_fusion = bf16[16,256,128]{2,1,0:T(8,128)(2,1)} fusion(f32[16,256,128]{2,1,0:T(8,128)S(1)} %fusion.26, bf16[128,16,256]{2,1,0:T(8,128)(2,1)S(1)} %fusion.6, bf16[128,128]{1,0:T(8,128)(2,1)S(1)} %copy-done.6), kind=kOutput, calls=%fused_computation.14 | convolution fusion | flops 136839168 | bytes 4227072 | tf_op jit(solution)/shard_map/hij,hc->ijc/dot_general | solution.py:18
  (16 shorter events, 0.1 us)
Async XLA Ops:
  6.5 99.4 %copy-start = (bf16[128,128]{1,0:T(8,128)(2,1)S(1)}, bf16[128,128]{1,0:T(8,128)(2,1)}, u32[]{:S(2)}) copy-start(bf16[128,128]{1,0:T(8,128)(2,1)} %param.19) | copy-start | bytes 98308
  6.5 4.1 %copy-start.2 = (bf16[16,256,128]{2,1,0:T(8,128)(2,1)S(1)}, bf16[16,256,128]{2,1,0:T(8,128)(2,1)}, u32[]{:S(2)}) copy-start(bf16[16,256,128]{2,1,0:T(8,128)(2,1)} %param.10) | copy-start | bytes 3145732
  6.5 4.1 %copy-start.5 = (f32[128]{0:T(128)S(1)}, f32[128]{0:T(128)}, u32[]{:S(2)}) copy-start(f32[128]{0:T(128)} %param.12) | copy-start | bytes 1540
  6.5 4.1 %copy-start.7 = (bf16[128,64]{0,1:T(8,128)(2,1)S(1)}, bf16[128,64]{0,1:T(8,128)(2,1)}, u32[]{:S(2)}) copy-start(bf16[128,64]{0,1:T(8,128)(2,1)} %param.15) | copy-start | bytes 49156
  6.5 92.9 %all-gather.3.cloned.1.call-start = ((), (), s32[]{:S(2)}) async-start(), calls=%async_computation | async-start | bytes 8912896 | tf_op jit(solution)/shard_map/all_gather | solution.py:52
  6.6 6.9 %copy-start.8 = (bf16[128,64]{0,1:T(8,128)(2,1)S(1)}, bf16[128,64]{0,1:T(8,128)(2,1)}, u32[]{:S(2)}) copy-start(bf16[128,64]{0,1:T(8,128)(2,1)} %param.16) | copy-start | bytes 49156
  10.7 5.6 %copy-start.3 = (s32[256]{0:T(256)S(1)}, s32[256]{0:T(256)}, u32[]{:S(2)}) copy-start(s32[256]{0:T(256)} %param.11) | copy-start | bytes 3076
  16.3 2.2 %copy-start.9 = (bf16[128,64]{0,1:T(8,128)(2,1)S(1)}, bf16[128,64]{0,1:T(8,128)(2,1)}, u32[]{:S(2)}) copy-start(bf16[128,64]{0,1:T(8,128)(2,1)} %param.13) | copy-start | bytes 49156
  18.4 2.9 %copy-start.10 = (bf16[128,64]{0,1:T(8,128)(2,1)S(1)}, bf16[128,64]{0,1:T(8,128)(2,1)}, u32[]{:S(2)}) copy-start(bf16[128,64]{0,1:T(8,128)(2,1)} %param.14) | copy-start | bytes 49156
  18.5 107.1 %all-gather.5.cloned.1.call-start = ((), (), s32[]{:S(2)}) async-start(), calls=%async_computation.1 | async-start | bytes 1572864 | tf_op jit(solution)/shard_map/all_gather | solution.py:59
  106.0 22.7 %copy-start.4 = (f32[128]{0:T(128)S(1)}, f32[128]{0:T(128)}, u32[]{:S(2)}) copy-start(f32[128]{0:T(128)} %param.17) | copy-start | bytes 1540
  107.5 21.6 %copy-start.6 = (bf16[128,128]{1,0:T(8,128)(2,1)S(1)}, bf16[128,128]{1,0:T(8,128)(2,1)}, u32[]{:S(2)}) copy-start(bf16[128,128]{1,0:T(8,128)(2,1)} %param.18) | copy-start | bytes 98308
  125.6 3.1 %copy-start.1 = (bf16[128,16,256]{2,1,0:T(8,128)(2,1)S(1)}, bf16[128,16,256]{2,1,0:T(8,128)(2,1)}, u32[]{:S(2)}) copy-start(bf16[128,16,256]{2,1,0:T(8,128)(2,1)} %all-gather.5.cloned.1.call-done) | copy-start | bytes 3145732
Sparse Core Ops, SparseCore 0:
  18.6 80.7 all-gather.2
  106.1 19.4 all-gather.4
where the time goes:
time: 138 us
  waiting for transfers between devices  93.4 us (68%)
  matrix products  21.1 us (15%)
  between operations  13.6 us (10%)
  other arithmetic  9.46 us (7%)
    all_gather x1, waiting for transfers between devices, body(): right_all = lax.all_gather(right, 'row', axis=1, tiled=True)  75.3 us
    all_gather x1, waiting for transfers between devices, body(): tri_full = lax.all_gather(tri_half, 'chan', axis=0, tiled=True)  18.1 us
    dot_general x1, matrix products, body(): lax.dot_general(left, right_all, (((2,), (2,)), ((0,), (0,))), preferred_...  6.51 us
    dot_general x2, matrix products, project(): jnp.einsum('ikc,ch->hik', normed, w_lin, preferred_element_type=jnp.float32)  5.57 us
    dot_general x2, matrix products, project(): jnp.einsum('ikc,ch->hik', normed, w_gate, preferred_element_type=jnp.floa...  5.57 us
    reduce_sum x2, other arithmetic, norm_axis(): variance = jnp.mean(centered * centered, axis=axis, keepdims=True)  3.89 us
    reduce_sum x2, other arithmetic, norm_axis(): mean = jnp.mean(values, axis=axis, keepdims=True)  3.16 us
  transfers between devices with their start and end apart: 2, of which 2 were waited for; matrix products, arithmetic and copies ran while one was open for 5% of the time, Pallas kernels for 0%

commit v1 on v0

v1 whole, which is shorter than its diff:
```python
import functools

import jax
import jax.numpy as jnp
from jax import lax
from jax.experimental import pallas as pl
from jax.experimental.pallas import tpu as pltpu
from jax.sharding import PartitionSpec as P

MESH = pl.DeviceIdType.MESH


def norm_axis(values, gain, axis):
    mean = jnp.mean(values, axis=axis, keepdims=True)
    centered = values - mean
    variance = jnp.mean(centered * centered, axis=axis, keepdims=True)
    return centered * lax.rsqrt(variance + 1e-05) * gain


def ring_orders(chunks, half):
    orders = []
    for way in range(2):
        order = []
        for first in range(0, chunks, 2):
            pair = [q for q in (first, first + 1) if q < chunks]
            block = [(q, d) for d in range(1, half + 1) for q in pair]
            block = [(q, d) for q, d in block if d < half or q % 2 == way]
            if order:
                tail = order.pop()
                order += [block[0], tail] + block[1:]
            else:
                order = block
        orders.append(order)
    return orders


def triangle_kernel(
    chips, chunks, left_ref, right_ref, tri_ref, held, lefts, part, sib_sem, ring_send, ring_recv, out_send, out_recv, local_sem
):
    rows = right_ref.shape[1]
    h_count = right_ref.shape[0]
    hc = h_count // chunks
    half = chips // 2
    index = lax.axis_index("row")
    x = lax.axis_index("chan")
    core = lax.rem(index, 2)
    chip = lax.div(index, 2)
    y = lax.rem(chip, 2)
    z = lax.div(chip, 2)
    place = jnp.where(y == 0, z, chips - 1 - z)

    def chip_at(ring_place):
        spot = lax.rem(ring_place + 2 * chips, chips)
        return jnp.where(spot < half, 2 * spot, 2 * (chips - 1 - spot) + 1)

    sibling = {"row": chip * 2 + (1 - core), "chan": x}
    nexts = [
        {"row": chip_at(place + 1) * 2 + core, "chan": x},
        {"row": chip_at(place - 1) * 2 + core, "chan": x},
    ]
    across = {"row": index, "chan": 1 - x}
    diagonal = {"row": chip * 2 + (1 - core), "chan": 1 - x}

    barrier = pltpu.get_barrier_semaphore()
    for partner in (sibling, nexts[0], nexts[1], across, diagonal):
        pl.semaphore_signal(barrier, inc=1, device_id=partner, device_id_type=MESH)
    pl.semaphore_wait(barrier, 5)

    def at_rows(block):
        return pl.ds(pl.multiple_of(block * rows, rows), rows)

    def ring_copy(way, q, d):
        step = 1 - 2 * way
        source = at_rows(chip_at(place - step * (d - 1)))
        heads = pl.ds(q * hc, hc)
        spot = held.at[heads, source]
        return pltpu.make_async_remote_copy(
            src_ref=right_ref.at[heads] if d == 1 else spot,
            dst_ref=spot,
            send_sem=ring_send.at[way, q, d - 1],
            recv_sem=ring_recv.at[way, q, d - 1],
            device_id=nexts[way],
            device_id_type=MESH,
        )

    left_copy = pltpu.make_async_remote_copy(
        src_ref=left_ref,
        dst_ref=lefts.at[:, at_rows(core)],
        send_sem=sib_sem.at[0],
        recv_sem=sib_sem.at[1],
        device_id=sibling,
        device_id_type=MESH,
    )

    def out_copies(q):
        heads = pl.ds(q * hc, hc)
        target = tri_ref.at[
            pl.ds(x * h_count + q * hc, hc), :, pl.ds(pl.multiple_of(core * rows * chips, 128), rows * chips)
        ]
        copies = []
        for n, (device, owner) in enumerate(((across, core), (diagonal, 1 - core), (sibling, 1 - core))):
            copies.append(
                pltpu.make_async_remote_copy(
                    src_ref=part.at[heads, at_rows(owner)],
                    dst_ref=target,
                    send_sem=out_send.at[n, q],
                    recv_sem=out_recv.at[n, q],
                    device_id=device,
                    device_id_type=MESH,
                )
            )
        own = pltpu.make_async_copy(part.at[heads, at_rows(core)], target, local_sem.at[q])
        return copies, own

    def compute(q):
        for way in range(2):
            top = half if q % 2 == way else half - 1
            for d in range(1, top + 1):
                if (way, q, d) not in waited:
                    ring_copy(way, q, d).wait_recv()
                    waited.add((way, q, d))
        heads = pl.ds(q * hc, hc)
        product = lax.dot_general(
            lefts[heads], held[heads], (((2,), (2,)), ((0,), (0,))), preferred_element_type=jnp.float32
        )
        part[heads] = product.astype(jnp.bfloat16)
        copies, own = out_copies(q)
        for copy in copies:
            copy.start()
        own.start()

    orders = ring_orders(chunks, half)
    waited = set()
    done = 0
    for n in range(len(orders[0])):
        for way in range(2):
            q, d = orders[way][n]
            if d > 1 and (way, q, d - 1) not in waited:
                ring_copy(way, q, d - 1).wait_recv()
                waited.add((way, q, d - 1))
            ring_copy(way, q, d).start()
        if n == 1:
            left_copy.start()
            held[:, at_rows(chip)] = right_ref[...]
            lefts[:, at_rows(core)] = left_ref[...]
        last = max(orders[w].index((done, half if done % 2 == w else half - 1)) for w in range(2))
        if n >= last + 2 and n < len(orders[0]) - 1:
            if done == 0:
                left_copy.wait_recv()
            compute(done)
            done += 1
    if done == 0:
        left_copy.wait_recv()
    while done < chunks:
        compute(done)
        done += 1
    for way in range(2):
        for q, d in orders[way]:
            ring_copy(way, q, d).wait_send()
    left_copy.wait_send()
    for q in range(chunks):
        copies, own = out_copies(q)
        for copy in copies:
            copy.wait()
        own.wait()


def triangle(left, right, row_devices, chunks):
    h_count, rows, depth = right.shape
    chips = row_devices // 2
    half = chips // 2
    dma = pltpu.SemaphoreType.DMA
    vmem = pl.BlockSpec(memory_space=pltpu.VMEM)
    return pl.pallas_call(
        functools.partial(triangle_kernel, chips, chunks),
        out_shape=jax.ShapeDtypeStruct((2 * h_count, rows, 2 * chips * rows), jnp.bfloat16),
        in_specs=[vmem, vmem],
        out_specs=vmem,
        scratch_shapes=[
            pltpu.VMEM((h_count, chips * rows, depth), jnp.bfloat16),
            pltpu.VMEM((h_count, 2 * rows, depth), jnp.bfloat16),
            pltpu.VMEM((h_count, 2 * rows, chips * rows), jnp.bfloat16),
            dma((2,)),
            dma((2, chunks, half)),
            dma((2, chunks, half)),
            dma((3, chunks)),
            dma((3, chunks)),
            dma((chunks,)),
        ],
        compiler_params=pltpu.CompilerParams(
            collective_id=0, has_side_effects=True, vmem_limit_bytes=40 * 1024 * 1024
        ),
        cost_estimate=pl.CostEstimate(
            flops=4 * h_count * rows * rows * chips * depth, bytes_accessed=8 * 1024 * 1024, transcendentals=0
        ),
    )(left, right)


def body(row_devices, chan_devices, sub_devices, *operands):
    pair_act, residue_valid, in_gain, w_left, w_left_gate, w_right, w_right_gate, out_gain, w_out, w_out_gate = operands
    row_count = pair_act.shape[0]
    col_count = pair_act.shape[1]
    row_first = lax.axis_index("row") * row_count
    col_first = lax.axis_index("sub") * col_count
    normed = norm_axis(pair_act.astype(jnp.float32), in_gain, 2).astype(jnp.bfloat16)
    valid = residue_valid.astype(jnp.float32)
    row_valid = lax.dynamic_slice_in_dim(valid, row_first, row_count)
    col_valid = lax.dynamic_slice_in_dim(valid, col_first, col_count)
    weight = (row_valid[:, None] * col_valid[None, :])[None, :, :]

    def project(w_lin, w_gate):
        linear = jnp.einsum("ikc,ch->hik", normed, w_lin, preferred_element_type=jnp.float32)
        gating = jnp.einsum("ikc,ch->hik", normed, w_gate, preferred_element_type=jnp.float32)
        return (jax.nn.sigmoid(gating) * linear * weight).astype(jnp.bfloat16)

    left = project(w_left, w_left_gate)
    right = project(w_right, w_right_gate)
    chips = row_devices // 2
    ringed = sub_devices == 1 and chan_devices == 2 and row_devices % 4 == 0 and (chips * row_count) % 128 == 0
    if ringed:
        tri_full = triangle(left, right, row_devices, 4)
    else:
        right_all = lax.all_gather(right, "row", axis=1, tiled=True)
        partial_tri = lax.dot_general(
            left, right_all, (((2,), (2,)), ((0,), (0,))), preferred_element_type=jnp.float32
        )
        tri_half = lax.psum_scatter(partial_tri.astype(jnp.bfloat16), "sub", scatter_dimension=2, tiled=True)
        tri_full = lax.all_gather(tri_half, "chan", axis=0, tiled=True)
    tri_norm = norm_axis(tri_full.astype(jnp.float32), out_gain[:, None, None], 0).astype(jnp.bfloat16)
    projected = jnp.einsum("hij,hc->ijc", tri_norm, w_out, preferred_element_type=jnp.float32)
    if ringed:
        split = projected.reshape(row_count, 2, chips, row_count, projected.shape[-1])
        projected = jnp.swapaxes(split, 1, 2).reshape(projected.shape)
    gating = jnp.einsum("ijc,cd->ijd", normed, w_out_gate, preferred_element_type=jnp.float32)
    return (jax.nn.sigmoid(gating) * projected).astype(jnp.bfloat16)


def solution(mesh):
    placed = (
        P(("groups", "row"), "sub", None),
        P("groups"),
        P(),
        P(None, "chan"),
        P(None, "chan"),
        P(None, "chan"),
        P(None, "chan"),
        P(),
        P(),
        P(),
    )
    return jax.shard_map(
        functools.partial(body, mesh.shape["row"], mesh.shape["chan"], mesh.shape["sub"]),
        mesh=mesh,
        in_specs=placed,
        out_specs=P(("groups", "row"), "sub", None),
        check_vma=False,
    )
```

time: 138 us -> 75.1 us (0.54)
  waiting for transfers between devices: 93.4 us -> 0 us
  Pallas kernels: 0 us -> 51.3 us
  between operations: 13.6 us -> 0.19 us
  matrix products: 21.1 us -> 14.2 us
    all_gather x2 -> x0, waiting for transfers between devices: 93.4 us -> none  [the longest x1 75.3 us: body(): right_all = lax.all_gather(right, 'row', axis=1, tiled=True)]
    pallas_call x0 -> x1, Pallas kernels: none -> 51.3 us  [triangle(): pl.pallas_call(functools.partial(triangle_kernel, chips, chunks), out_sha...]
    dot_general x3 -> x2, matrix products: 9.92 us -> 3.01 us  [the longest x1 2.46 us: body(): jnp.einsum('ijc,cd->ijd', normed, w_out_gate, preferred_element_type=jnp....]
  transfers between devices with their start and end apart: 2 -> 0, of which waited for: 2 -> 0; matrix products, arithmetic and copies ran while one was open for 5% -> 0% of each run, Pallas kernels for 0% -> 0%
where the time goes in v1:
time: 75.1 us; the launch traced here: 74.8 us
  Pallas kernels  51.3 us (68%)
  matrix products  14.2 us (19%)
  other arithmetic  8.25 us (11%)
  local copies, waits for them, and re-layouts  0.86 us (1%)
    pallas_call x1, Pallas kernels, triangle(): pl.pallas_call(functools.partial(triangle_kernel, chips, chunks), out_sha...  51.3 us
    dot_general x2, matrix products, project(): jnp.einsum('ikc,ch->hik', normed, w_gate, preferred_element_type=jnp.floa...  5.57 us
    dot_general x2, matrix products, project(): jnp.einsum('ikc,ch->hik', normed, w_lin, preferred_element_type=jnp.float32)  5.57 us
    reduce_sum x2, other arithmetic, norm_axis(): variance = jnp.mean(centered * centered, axis=axis, keepdims=True)  2.66 us
    convert_element_type x1, other arithmetic, project(): return (jax.nn.sigmoid(gating) * linear * weight).astype(jnp.bfloat16)  2.6 us
    dot_general x1, matrix products, body(): jnp.einsum('ijc,cd->ijd', normed, w_out_gate, preferred_element_type=jnp....  2.46 us
    reduce_sum x2, other arithmetic, norm_axis(): mean = jnp.mean(values, axis=axis, keepdims=True)  1.78 us

profile of v1, /device:TPU:0, one launch (start us, length us, event | category | flops | bytes accessed | tf_op | source)
XLA Modules:
  0.0 74.8 jit_solution(10158352830789233437)
XLA Ops:
  0.0 0.0 copy-start
  0.0 0.0 copy-start.1
  0.0 0.8 %convert_element_type.26 = f32[256]{0:T(256)S(1)} convert(s32[256]{0:T(256)} %param.11) | non-fusion elementwise | flops 256 | bytes 2048 | tf_op jit(solution)/shard_map/convert_element_type | solution.py:206
  0.8 0.1 dynamic_slice.4
  0.9 0.1 broadcast_multiply_fusion
  0.9 1.6 %convert_reduce_fusion.1 = f32[16,256]{1,0:T(8,128)S(1)} fusion(bf16[16,256,128]{2,1,0:T(8,128)(2,1)} %param.10), kind=kLoop, calls=%fused_computation.3 | loop fusion | flops 1044480 | bytes 1064960 | tf_op jit(solution)/shard_map/reduce_sum | solution.py:14
  2.5 2.3 %fusion.7 = f32[16,256]{1,0:T(8,128)S(1)} fusion(bf16[16,256,128]{2,1,0:T(8,128)(2,1)} %param.10, f32[16,256]{1,0:T(8,128)S(1)} %broadcast_multiply_fusion.2), kind=kLoop, calls=%fused_computation.11 | loop fusion | flops 2093056 | bytes 1081344 | tf_op jit(solution)/shard_map/reduce_sum | solution.py:16
  4.9 0.0 copy-done.1
  4.9 0.0 copy-done.8
  4.9 0.0 copy-done.4
  4.9 0.0 copy-start.6
  4.9 2.8 %fusion.33 = f32[16,256,64]{1,2,0:T(8,128)S(1)} fusion(bf16[128,64]{0,1:T(8,128)(2,1)S(1)} %copy-done.4, bf16[16,256,128]{2,1,0:T(8,128)(2,1)S(1)} %copy-done.1, f32[128]{0:T(128)S(1)} %copy-done.8, f32[16,256]{1,0:T(8,128)S(1)} %add_rsqrt_fusion.1, f32[16,256]{1,0:T(8,128)S(1)} %broadcast_multiply_fusion.2), kind=kOutput, calls=%fused_computation.42 | convolution fusion | flops 69730304 | bytes 2146816 | tf_op jit(solution)/shard_map/ikc,ch->hik/dot_general | solution.py:213
  7.7 0.0 copy-done.5
  7.7 0.0 copy-start.7
  7.8 2.8 %fusion.31 = f32[16,256,64]{1,2,0:T(8,128)S(1)} fusion(bf16[128,64]{0,1:T(8,128)(2,1)S(1)} %copy-done.5, bf16[16,256,128]{2,1,0:T(8,128)(2,1)S(1)} %copy-done.1, f32[128]{0:T(128)S(1)} %copy-done.8, f32[16,256]{1,0:T(8,128)S(1)} %add_rsqrt_fusion.1, f32[16,256]{1,0:T(8,128)S(1)} %broadcast_multiply_fusion.2), kind=kOutput, calls=%fused_computation.40 | convolution fusion | flops 69730304 | bytes 2146816 | tf_op jit(solution)/shard_map/ikc,ch->hik/dot_general | solution.py:212
  10.6 0.0 copy-done.6
  10.6 2.8 %fusion.29 = f32[16,256,64]{1,2,0:T(8,128)S(1)} fusion(bf16[128,64]{0,1:T(8,128)(2,1)S(1)} %copy-done.6, bf16[16,256,128]{2,1,0:T(8,128)(2,1)S(1)} %copy-done.1, f32[128]{0:T(128)S(1)} %copy-done.8, f32[16,256]{1,0:T(8,128)S(1)} %add_rsqrt_fusion.1, f32[16,256]{1,0:T(8,128)S(1)} %broadcast_multiply_fusion.2), kind=kOutput, calls=%fused_computation.38 | convolution fusion | flops 69730304 | bytes 2146816 | tf_op jit(solution)/shard_map/ikc,ch->hik/dot_general | solution.py:213
  13.4 0.0 copy-done.7
  13.4 2.8 %fusion.27 = f32[16,256,64]{1,2,0:T(8,128)S(1)} fusion(bf16[128,64]{0,1:T(8,128)(2,1)S(1)} %copy-done.7, bf16[16,256,128]{2,1,0:T(8,128)(2,1)S(1)} %copy-done.1, f32[128]{0:T(128)S(1)} %copy-done.8, f32[16,256]{1,0:T(8,128)S(1)} %add_rsqrt_fusion.1, f32[16,256]{1,0:T(8,128)S(1)} %broadcast_multiply_fusion.2), kind=kOutput, calls=%fused_computation.36 | convolution fusion | flops 69730304 | bytes 2146816 | tf_op jit(solution)/shard_map/ikc,ch->hik/dot_general | solution.py:212
  16.2 2.6 %fusion.24 = (bf16[64,16,256]{2,1,0:T(8,128)(2,1)S(1)}, bf16[64,16,256]{2,1,0:T(8,128)(2,1)S(1)}) fusion(f32[16,256]{1,0:T(8,128)S(1)} %broadcast_multiply_fusion, f32[16,256,64]{1,2,0:T(8,128)S(1)} %fusion.27, f32[16,256,64]{1,2,0:T(8,128)S(1)} %fusion.29, f32[16,256,64]{1,2,0:T(8,128)S(1)} %fusion.31, f32[16,256,64]{1,2,0:T(8,128)S(1)} %fusion.33), kind=kLoop, calls=%fused_computation.33 | loop fusion | flops 3145728 | bytes 5259264 | tf_op jit(solution)/shard_map/convert_element_type | solution.py:214
  18.8 0.0 copy-start.2
  18.8 51.3 %shard_map.100 = bf16[128,16,256]{2,1,0:T(8,128)(2,1)S(1)} custom-call(bf16[64,16,256]{2,1,0:T(8,128)(2,1)S(1)} %get-tuple-element.6.left_ref, bf16[64,16,256]{2,1,0:T(8,128)(2,1)S(1)} %get-tuple-element.5.right_ref), custom_call_target="tpu_custom_call" | custom-call | flops 134217728 | bytes 8388608 | tf_op jit(solution)/shard_map/pallas_call | solution.py:174
  70.1 0.2 convert_reduce_fusion
  70.3 0.3 fusion.4
  70.7 0.0 copy-done.2
  70.7 0.3 fusion.6
  71.0 0.0 copy-done
  71.0 0.6 fusion.11
  71.6 0.0 copy-start.3
  71.6 0.3 copy.16
  71.9 0.5 copy-done.3
  72.3 2.5 %fusion.10 = bf16[16,256,128]{2,1,0:T(8,128)(2,1)} fusion(f32[16,2,8,16,128]{4,3,1,2,0:T(8,128)S(1)} %copy.16, bf16[128,128]{1,0:T(8,128)(2,1)S(1)} %copy-done.3, bf16[16,256,128]{2,1,0:T(8,128)(2,1)S(1)} %copy-done.1, f32[128]{0:T(128)S(1)} %copy-done.8, f32[16,256]{1,0:T(8,128)S(1)} %add_rsqrt_fusion.1, f32[16,256]{1,0:T(8,128)S(1)} %broadcast_multiply_fusion.2), kind=kOutput, calls=%fused_computation.15 | convolution fusion | flops 139460608 | bytes 4260352 | tf_op jit(solution)/shard_map/ijc,cd->ijd/dot_general | solution.py:234
  (7 shorter events, 0.0 us)
Async XLA Ops:
  0.0 71.0 %copy-start = (bf16[128,128]{1,0:T(8,128)(2,1)S(1)}, bf16[128,128]{1,0:T(8,128)(2,1)}, u32[]{:S(2)}) copy-start(bf16[128,128]{1,0:T(8,128)(2,1)} %param.18) | copy-start | bytes 98308
  0.0 4.9 %copy-start.1 = (bf16[16,256,128]{2,1,0:T(8,128)(2,1)S(1)}, bf16[16,256,128]{2,1,0:T(8,128)(2,1)}, u32[]{:S(2)}) copy-start(bf16[16,256,128]{2,1,0:T(8,128)(2,1)} %param.10) | copy-start | bytes 3145732
  0.0 4.9 %copy-start.8 = (f32[128]{0:T(128)S(1)}, f32[128]{0:T(128)}, u32[]{:S(2)}) copy-start(f32[128]{0:T(128)} %param.12) | copy-start | bytes 1540
  0.0 4.9 %copy-start.4 = (bf16[128,64]{0,1:T(8,128)(2,1)S(1)}, bf16[128,64]{0,1:T(8,128)(2,1)}, u32[]{:S(2)}) copy-start(bf16[128,64]{0,1:T(8,128)(2,1)} %param.14) | copy-start | bytes 49156
  0.9 6.8 %copy-start.5 = (bf16[128,64]{0,1:T(8,128)(2,1)S(1)}, bf16[128,64]{0,1:T(8,128)(2,1)}, u32[]{:S(2)}) copy-start(bf16[128,64]{0,1:T(8,128)(2,1)} %param.13) | copy-start | bytes 49156
  4.9 5.6 %copy-start.6 = (bf16[128,64]{0,1:T(8,128)(2,1)S(1)}, bf16[128,64]{0,1:T(8,128)(2,1)}, u32[]{:S(2)}) copy-start(bf16[128,64]{0,1:T(8,128)(2,1)} %param.16) | copy-start | bytes 49156
  7.7 5.6 %copy-start.7 = (bf16[128,64]{0,1:T(8,128)(2,1)S(1)}, bf16[128,64]{0,1:T(8,128)(2,1)}, u32[]{:S(2)}) copy-start(bf16[128,64]{0,1:T(8,128)(2,1)} %param.15) | copy-start | bytes 49156
  18.8 51.9 %copy-start.2 = (f32[128]{0:T(128)S(1)}, f32[128]{0:T(128)}, u32[]{:S(2)}) copy-start(f32[128]{0:T(128)} %param.17) | copy-start | bytes 1540
  71.6 0.8 %copy-start.3 = (bf16[128,128]{1,0:T(8,128)(2,1)S(1)}, bf16[128,128]{1,0:T(8,128)(2,1)}, u32[]{:S(2)}) copy-start(bf16[128,128]{1,0:T(8,128)(2,1)} %param.19) | copy-start | bytes 98308

commit v2 on v1

v2 whole, which is shorter than its diff:
```python
import functools

import jax
import jax.numpy as jnp
from jax import lax
from jax.experimental import pallas as pl
from jax.experimental.pallas import tpu as pltpu
from jax.sharding import PartitionSpec as P

MESH = pl.DeviceIdType.MESH


def norm_axis(values, gain, axis):
    mean = jnp.mean(values, axis=axis, keepdims=True)
    centered = values - mean
    variance = jnp.mean(centered * centered, axis=axis, keepdims=True)
    return centered * lax.rsqrt(variance + 1e-05) * gain


def ring_orders(chunks, half):
    orders = []
    for way in range(2):
        order = []
        for first in range(0, chunks, 2):
            pair = [q for q in (first, first + 1) if q < chunks]
            block = [(q, d) for d in range(1, half + 1) for q in pair]
            block = [(q, d) for q, d in block if d < half or q % 2 == way]
            if order:
                tail = order.pop()
                order += [block[0], tail] + block[1:]
            else:
                order = block
        orders.append(order)
    return orders


def triangle_kernel(
    chips,
    chunks,
    pair_ref,
    row_valid_ref,
    col_valid_ref,
    in_gain_ref,
    w_left_ref,
    w_left_gate_ref,
    w_right_ref,
    w_right_gate_ref,
    w_out_gate_ref,
    tri_ref,
    gate_ref,
    normed,
    weights,
    staged,
    held,
    lefts,
    part,
    sib_sem,
    ring_send,
    ring_recv,
    out_send,
    out_recv,
    local_sem,
):
    rows = pair_ref.shape[0]
    h_count = w_left_ref.shape[0]
    hc = h_count // chunks
    half = chips // 2
    index = lax.axis_index("row")
    x = lax.axis_index("chan")
    core = lax.rem(index, 2)
    chip = lax.div(index, 2)
    y = lax.rem(chip, 2)
    z = lax.div(chip, 2)
    place = jnp.where(y == 0, z, chips - 1 - z)

    def chip_at(ring_place):
        spot = lax.rem(ring_place + 2 * chips, chips)
        return jnp.where(spot < half, 2 * spot, 2 * (chips - 1 - spot) + 1)

    sibling = {"row": chip * 2 + (1 - core), "chan": x}
    nexts = [
        {"row": chip_at(place + 1) * 2 + core, "chan": x},
        {"row": chip_at(place - 1) * 2 + core, "chan": x},
    ]
    across = {"row": index, "chan": 1 - x}
    diagonal = {"row": chip * 2 + (1 - core), "chan": 1 - x}

    barrier = pltpu.get_barrier_semaphore()
    for partner in (sibling, nexts[0], nexts[1], across, diagonal):
        pl.semaphore_signal(barrier, inc=1, device_id=partner, device_id_type=MESH)

    def at_rows(block):
        return pl.ds(pl.multiple_of(block * rows, rows), rows)

    def at_heads(q):
        return pl.ds(q * hc, hc)

    weights[0, :h_count] = w_right_ref[...]
    weights[0, h_count:] = w_right_gate_ref[...]
    weights[1, :h_count] = w_left_ref[...]
    weights[1, h_count:] = w_left_gate_ref[...]
    col_valid = col_valid_ref[...].astype(jnp.float32)

    def project(i, side, block):
        both = lax.dot_general(
            weights[side], block, (((1,), (1,)), ((), ())), preferred_element_type=jnp.float32
        )
        weight = col_valid * row_valid_ref[index * rows + i].astype(jnp.float32)
        staged[side, i] = jax.nn.sigmoid(both[h_count:]) * both[:h_count] * weight

    def right_row(i, carry):
        values = pair_ref[i].astype(jnp.float32)
        mean = jnp.mean(values, axis=1, keepdims=True)
        centered = values - mean
        variance = jnp.mean(centered * centered, axis=1, keepdims=True)
        block = (centered * lax.rsqrt(variance + 1e-05) * in_gain_ref[...]).astype(jnp.bfloat16)
        normed[i] = block
        project(i, 0, block)
        return carry

    def left_row(i, carry):
        project(i, 1, normed[i])
        return carry

    def gate_row(i, carry):
        gate_ref[i] = jax.nn.sigmoid(
            jnp.dot(normed[i], w_out_gate_ref[...], preferred_element_type=jnp.float32)
        )
        return carry

    def turned(side, q):
        return jnp.swapaxes(staged[side, :, q * hc : (q + 1) * hc, :], 0, 1).astype(jnp.bfloat16)

    def turn_right(q):
        held[at_heads(q), at_rows(chip)] = turned(0, q)

    def ring_copy(way, q, d):
        step = 1 - 2 * way
        spot = held.at[at_heads(q), at_rows(chip_at(place - step * (d - 1)))]
        return pltpu.make_async_remote_copy(
            src_ref=spot,
            dst_ref=spot,
            send_sem=ring_send.at[way, q, d - 1],
            recv_sem=ring_recv.at[way, q, d - 1],
            device_id=nexts[way],
            device_id_type=MESH,
        )

    left_spot = lefts.at[:, at_rows(core)]
    left_copy = pltpu.make_async_remote_copy(
        src_ref=left_spot,
        dst_ref=left_spot,
        send_sem=sib_sem.at[0],
        recv_sem=sib_sem.at[1],
        device_id=sibling,
        device_id_type=MESH,
    )

    def send_left():
        for q in range(chunks):
            lefts[at_heads(q), at_rows(core)] = turned(1, q)
        left_copy.start()

    def out_copies(q):
        target = tri_ref.at[
            pl.ds(x * h_count + q * hc, hc), :, pl.ds(pl.multiple_of(core * rows * chips, 128), rows * chips)
        ]
        copies = []
        for n, (device, owner) in enumerate(((across, core), (diagonal, 1 - core), (sibling, 1 - core))):
            copies.append(
                pltpu.make_async_remote_copy(
                    src_ref=part.at[at_heads(q), at_rows(owner)],
                    dst_ref=target,
                    send_sem=out_send.at[n, q],
                    recv_sem=out_recv.at[n, q],
                    device_id=device,
                    device_id_type=MESH,
                )
            )
        own = pltpu.make_async_copy(part.at[at_heads(q), at_rows(core)], target, local_sem.at[q])
        return copies, own

    waited = set()

    def arrived(way, q, d):
        if (way, q, d) not in waited:
            ring_copy(way, q, d).wait_recv()
            waited.add((way, q, d))

    def compute(q):
        for way in range(2):
            top = half if q % 2 == way else half - 1
            for d in range(1, top + 1):
                arrived(way, q, d)
        heads = at_heads(q)
        product = lax.dot_general(
            lefts[heads], held[heads], (((2,), (2,)), ((0,), (0,))), preferred_element_type=jnp.float32
        )
        part[heads] = product.astype(jnp.bfloat16)
        copies, own = out_copies(q)
        for copy in copies:
            copy.start()
        own.start()

    lax.fori_loop(0, rows, right_row, 0)
    quarter = rows // 4
    tasks = [functools.partial(turn_right, q) for q in range(2, chunks)]
    tasks += [functools.partial(lax.fori_loop, n * quarter, (n + 1) * quarter, left_row, 0) for n in range(4)]
    tasks += [send_left]
    tasks += [functools.partial(lax.fori_loop, n * quarter, (n + 1) * quarter, gate_row, 0) for n in range(4)]

    orders = ring_orders(chunks, half)
    steps = len(orders[0])
    done = 0
    for n in range(steps):
        if n < 2:
            turn_right(n)
        if n == 0:
            pl.semaphore_wait(barrier, 5)
        for way in range(2):
            q, d = orders[way][n]
            if d > 1:
                arrived(way, q, d - 1)
            ring_copy(way, q, d).start()
        if n >= 1:
            for task in tasks[:2]:
                task()
            tasks = tasks[2:]
        last = max(orders[w].index((done, half if done % 2 == w else half - 1)) for w in range(2))
        if n >= last + 2 and n < steps - 1 and not tasks:
            if done == 0:
                left_copy.wait_recv()
            compute(done)
            done += 1
    for task in tasks:
        task()
    if done == 0:
        left_copy.wait_recv()
    while done < chunks:
        compute(done)
        done += 1
    for way in range(2):
        for q, d in orders[way]:
            ring_copy(way, q, d).wait_send()
    left_copy.wait_send()
    for q in range(chunks):
        copies, own = out_copies(q)
        for copy in copies:
            copy.wait()
        own.wait()


def triangle(chips, chunks, pair_act, residue_valid, in_gain, w_left, w_left_gate, w_right, w_right_gate, w_out_gate):
    rows, depth, channels = pair_act.shape
    h_count = w_left.shape[1]
    half = chips // 2
    dma = pltpu.SemaphoreType.DMA
    vmem = pl.BlockSpec(memory_space=pltpu.VMEM)
    smem = pl.BlockSpec(memory_space=pltpu.SMEM)
    return pl.pallas_call(
        functools.partial(triangle_kernel, chips, chunks),
        out_shape=[
            jax.ShapeDtypeStruct((2 * h_count, rows, chips * 2 * rows), jnp.bfloat16),
            jax.ShapeDtypeStruct((rows, depth, w_out_gate.shape[1]), jnp.float32),
        ],
        in_specs=[vmem, smem] + [vmem] * 7,
        out_specs=[vmem, vmem],
        scratch_shapes=[
            pltpu.VMEM((rows, depth, channels), jnp.bfloat16),
            pltpu.VMEM((2, 2 * h_count, channels), jnp.bfloat16),
            pltpu.VMEM((2, rows, h_count, depth), jnp.float32),
            pltpu.VMEM((h_count, chips * rows, depth), jnp.bfloat16),
            pltpu.VMEM((h_count, 2 * rows, depth), jnp.bfloat16),
            pltpu.VMEM((h_count, 2 * rows, chips * rows), jnp.bfloat16),
            dma((2,)),
            dma((2, chunks, half)),
            dma((2, chunks, half)),
            dma((3, chunks)),
            dma((3, chunks)),
            dma((chunks,)),
        ],
        compiler_params=pltpu.CompilerParams(
            collective_id=0, has_side_effects=True, vmem_limit_bytes=48 * 1024 * 1024
        ),
    )(
        pair_act,
        residue_valid,
        residue_valid[None, :],
        in_gain[None, :],
        w_left.T,
        w_left_gate.T,
        w_right.T,
        w_right_gate.T,
        w_out_gate,
    )


def finish(tri_full, out_gain, w_out):
    tri_norm = norm_axis(tri_full.astype(jnp.float32), out_gain[:, None, None], 0).astype(jnp.bfloat16)
    return jnp.einsum("hij,hc->ijc", tri_norm, w_out, preferred_element_type=jnp.float32)


def ring_body(chips, *operands):
    out_gain, w_out, w_out_gate = operands[-3:]
    tri_full, gate = triangle(chips, 4, *operands[:-3], w_out_gate)
    projected = finish(tri_full, out_gain, w_out)
    rows = operands[0].shape[0]
    split = projected.reshape(rows, 2, chips, rows, projected.shape[-1])
    return (gate * jnp.swapaxes(split, 1, 2).reshape(projected.shape)).astype(jnp.bfloat16)


def body(*operands):
    pair_act, residue_valid, in_gain, w_left, w_left_gate, w_right, w_right_gate, out_gain, w_out, w_out_gate = operands
    row_count = pair_act.shape[0]
    col_count = pair_act.shape[1]
    row_first = lax.axis_index("row") * row_count
    col_first = lax.axis_index("sub") * col_count
    normed = norm_axis(pair_act.astype(jnp.float32), in_gain, 2).astype(jnp.bfloat16)
    valid = residue_valid.astype(jnp.float32)
    row_valid = lax.dynamic_slice_in_dim(valid, row_first, row_count)
    col_valid = lax.dynamic_slice_in_dim(valid, col_first, col_count)
    weight = (row_valid[:, None] * col_valid[None, :])[None, :, :]

    def project(w_lin, w_gate):
        linear = jnp.einsum("ikc,ch->hik", normed, w_lin, preferred_element_type=jnp.float32)
        gating = jnp.einsum("ikc,ch->hik", normed, w_gate, preferred_element_type=jnp.float32)
        return (jax.nn.sigmoid(gating) * linear * weight).astype(jnp.bfloat16)

    left = project(w_left, w_left_gate)
    right = project(w_right, w_right_gate)
    right_all = lax.all_gather(right, "row", axis=1, tiled=True)
    partial_tri = lax.dot_general(
        left, right_all, (((2,), (2,)), ((0,), (0,))), preferred_element_type=jnp.float32
    )
    tri_half = lax.psum_scatter(partial_tri.astype(jnp.bfloat16), "sub", scatter_dimension=2, tiled=True)
    tri_full = lax.all_gather(tri_half, "chan", axis=0, tiled=True)
    gating = jnp.einsum("ijc,cd->ijd", normed, w_out_gate, preferred_element_type=jnp.float32)
    return (jax.nn.sigmoid(gating) * finish(tri_full, out_gain, w_out)).astype(jnp.bfloat16)


def solution(mesh):
    placed = (
        P(("groups", "row"), "sub", None),
        P("groups"),
        P(),
        P(None, "chan"),
        P(None, "chan"),
        P(None, "chan"),
        P(None, "chan"),
        P(),
        P(),
        P(),
    )
    rows, chan, sub = (mesh.shape[name] for name in ("row", "chan", "sub"))
    ringed = sub == 1 and chan == 2 and rows % 8 == 0
    return jax.shard_map(
        functools.partial(ring_body, rows // 2) if ringed else body,
        mesh=mesh,
        in_specs=placed,
        out_specs=P(("groups", "row"), "sub", None),
        check_vma=False,
    )
```

time: 75.1 us -> 66 us (0.88)
  matrix products: 14.2 us -> 0.55 us
  other arithmetic: 8.25 us -> 2.09 us
  local copies, waits for them, and re-layouts: 0.86 us -> 6.47 us
  Pallas kernels: 51.3 us -> 56.2 us
    dot_general x6 -> x1, matrix products: 14.2 us -> 0.55 us  [finish(): jnp.einsum('hij,hc->ijc', tri_norm, w_out, preferred_element_type=jnp.flo...]
    unnamed x18 -> x20, local copies, waits for them, and re-layouts: 0.52 us -> 6.21 us
    pallas_call x1, Pallas kernels: 51.3 us -> 56.2 us  [triangle(): pl.pallas_call(functools.partial(triangle_kernel, chips, chunks), out_sha...]
    reduce_sum x2 -> x1, other arithmetic: 2.66 us -> 0.33 us  [norm_axis(): variance = jnp.mean(centered * centered, axis=axis, keepdims=True)]
    convert_element_type x3 -> x2, other arithmetic: 3.7 us -> 1.55 us  [the longest x1 1.22 us: ring_body(): (gate * jnp.swapaxes(split, 1, 2).reshape(projected.shape)).astype(jnp.bf...]
    reduce_sum x2 -> x1, other arithmetic: 1.78 us -> 0.2 us  [norm_axis(): mean = jnp.mean(values, axis=axis, keepdims=True)]
where the time goes in v2:
time: 66 us; the launch traced here: 65.4 us
  Pallas kernels  56.2 us (85%)
  local copies, waits for them, and re-layouts  6.47 us (10%)
  other arithmetic  2.09 us (3%)
    pallas_call x1, Pallas kernels, triangle(): pl.pallas_call(functools.partial(triangle_kernel, chips, chunks), out_sha...  56.2 us
    unnamed x20, local copies, waits for them, and re-layouts  6.21 us

profile of v2, /device:TPU:0, one launch (start us, length us, event | category | flops | bytes accessed | tf_op | source)
XLA Modules:
  0.0 65.4 jit_solution(7946044258260546846)
XLA Ops:
  0.0 0.0 copy-start
  0.0 0.0 copy-start.9
  0.0 0.0 copy-start.1
  0.0 1.2 %copy-done.1 = bf16[16,256,128]{2,1,0:T(8,128)(2,1)S(1)} copy-done((bf16[16,256,128]{2,1,0:T(8,128)(2,1)S(1)}, bf16[16,256,128]{2,1,0:T(8,128)(2,1)}, u32[]{:S(2)}) %copy-start.1) | copy-done | bytes 1048600
  1.3 0.0 copy-start.2
  1.3 0.8 %copy-done.2 = bf16[128,128]{1,0:T(8,128)(2,1)S(1)} copy-done((bf16[128,128]{1,0:T(8,128)(2,1)S(1)}, bf16[128,128]{1,0:T(8,128)(2,1)}, u32[]{:S(2)}) %copy-start.2) | copy-done | bytes 32792
  2.0 0.0 copy-start.3
  2.0 0.7 %copy-done.3 = bf16[128,64]{0,1:T(8,128)(2,1)S(1)} copy-done((bf16[128,64]{0,1:T(8,128)(2,1)S(1)}, bf16[128,64]{0,1:T(8,128)(2,1)}, u32[]{:S(2)}) %copy-start.3) | copy-done | bytes 16408
  2.7 0.0 copy-start.4
  2.7 0.7 %copy-done.4 = bf16[128,64]{0,1:T(8,128)(2,1)S(1)} copy-done((bf16[128,64]{0,1:T(8,128)(2,1)S(1)}, bf16[128,64]{0,1:T(8,128)(2,1)}, u32[]{:S(2)}) %copy-start.4) | copy-done | bytes 16408
  3.4 0.0 copy-start.5
  3.4 0.7 %copy-done.5 = bf16[128,64]{0,1:T(8,128)(2,1)S(1)} copy-done((bf16[128,64]{0,1:T(8,128)(2,1)S(1)}, bf16[128,64]{0,1:T(8,128)(2,1)}, u32[]{:S(2)}) %copy-start.5) | copy-done | bytes 16408
  4.2 0.0 copy-start.6
  4.2 0.7 %copy-done.6 = bf16[128,64]{0,1:T(8,128)(2,1)S(1)} copy-done((bf16[128,64]{0,1:T(8,128)(2,1)S(1)}, bf16[128,64]{0,1:T(8,128)(2,1)}, u32[]{:S(2)}) %copy-start.6) | copy-done | bytes 16408
  4.9 0.0 copy-start.7
  4.9 0.7 %copy-done.7 = s32[256]{0:T(256)S(1)} copy-done((s32[256]{0:T(256)S(1)}, s32[256]{0:T(256)}, u32[]{:S(2)}) %copy-start.7) | copy-done | bytes 1048
  5.6 0.0 copy-start.8
  5.6 0.7 copy-done.8
  6.2 56.2 %shard_map.100 = (bf16[128,16,256]{2,1,0:T(8,128)(2,1)S(1)}, f32[16,256,128]{2,1,0:T(8,128)S(1)}) custom-call(bf16[16,256,128]{2,1,0:T(8,128)(2,1)S(1)} %copy-done.1, s32[256]{0:T(256)S(1)} %copy-done.7, s32[1,256]{1,0:T(1,128)S(1)} %bitcast.20, f32[1,128]{1,0:T(1,128)S(1)} %bitcast.21, bf16[64,128]{1,0:T(8,128)(2,1)S(1)} %bitcast.16, ...), custom_call_target="tpu_custom_call" | custom-call | tf_op jit(solution)/shard_map/pallas_call | solution.py:260
  62.4 0.2 convert_reduce_fusion
  62.6 0.3 fusion.2
  63.0 0.0 copy-done.9
  63.0 0.3 fusion.4
  63.3 0.0 copy-done
  63.3 0.6 fusion.6
  63.9 0.3 copy.12
  64.1 1.2 %fusion.5 = bf16[16,256,128]{2,1,0:T(8,128)(2,1)} fusion(f32[16,256,128]{2,1,0:T(8,128)S(1)} %get-tuple-element.7, f32[16,2,8,16,128]{4,3,1,2,0:T(8,128)S(1)} %copy.12), kind=kLoop, calls=%fused_computation.8 | loop fusion | flops 1048576 | bytes 5242880 | tf_op jit(solution)/shard_map/convert_element_type | solution.py:309
  (2 shorter events, 0.0 us)
Async XLA Ops:
  0.0 63.3 %copy-start = (bf16[128,128]{1,0:T(8,128)(2,1)S(1)}, bf16[128,128]{1,0:T(8,128)(2,1)}, u32[]{:S(2)}) copy-start(bf16[128,128]{1,0:T(8,128)(2,1)} %param.18) | copy-start | bytes 98308
  0.0 63.0 %copy-start.9 = (f32[128]{0:T(128)S(1)}, f32[128]{0:T(128)}, u32[]{:S(2)}) copy-start(f32[128]{0:T(128)} %param.17) | copy-start | bytes 1540
  0.0 1.2 %copy-start.1 = (bf16[16,256,128]{2,1,0:T(8,128)(2,1)S(1)}, bf16[16,256,128]{2,1,0:T(8,128)(2,1)}, u32[]{:S(2)}) copy-start(bf16[16,256,128]{2,1,0:T(8,128)(2,1)} %pair_ref.1) | copy-start | bytes 3145732
  1.3 0.8 %copy-start.2 = (bf16[128,128]{1,0:T(8,128)(2,1)S(1)}, bf16[128,128]{1,0:T(8,128)(2,1)}, u32[]{:S(2)}) copy-start(bf16[128,128]{1,0:T(8,128)(2,1)} %w_out_gate_ref.1) | copy-start | bytes 98308
  2.0 0.7 %copy-start.3 = (bf16[128,64]{0,1:T(8,128)(2,1)S(1)}, bf16[128,64]{0,1:T(8,128)(2,1)}, u32[]{:S(2)}) copy-start(bf16[128,64]{0,1:T(8,128)(2,1)} %param.13) | copy-start | bytes 49156
  2.7 0.7 %copy-start.4 = (bf16[128,64]{0,1:T(8,128)(2,1)S(1)}, bf16[128,64]{0,1:T(8,128)(2,1)}, u32[]{:S(2)}) copy-start(bf16[128,64]{0,1:T(8,128)(2,1)} %param.14) | copy-start | bytes 49156
  3.4 0.7 %copy-start.5 = (bf16[128,64]{0,1:T(8,128)(2,1)S(1)}, bf16[128,64]{0,1:T(8,128)(2,1)}, u32[]{:S(2)}) copy-start(bf16[128,64]{0,1:T(8,128)(2,1)} %param.15) | copy-start | bytes 49156
  4.2 0.7 %copy-start.6 = (bf16[128,64]{0,1:T(8,128)(2,1)S(1)}, bf16[128,64]{0,1:T(8,128)(2,1)}, u32[]{:S(2)}) copy-start(bf16[128,64]{0,1:T(8,128)(2,1)} %param.16) | copy-start | bytes 49156
  4.9 0.7 %copy-start.7 = (s32[256]{0:T(256)S(1)}, s32[256]{0:T(256)}, u32[]{:S(2)}) copy-start(s32[256]{0:T(256)} %row_valid_ref.1) | copy-start | bytes 3076
  5.6 0.7 %copy-start.8 = (f32[128]{0:T(128)S(1)}, f32[128]{0:T(128)}, u32[]{:S(2)}) copy-start(f32[128]{0:T(128)} %param.12) | copy-start | bytes 1540

commit v3 on v2

--- a/solution.py
+++ b/solution.py
@@ -37,17 +37,23 @@
 def triangle_kernel(
     chips,
     chunks,
+    row_valid_ref,
+    pair_hbm,
+    col_valid_hbm,
+    in_gain_hbm,
+    w_left_hbm,
+    w_left_gate_hbm,
+    w_right_hbm,
+    w_right_gate_hbm,
+    w_out_gate_hbm,
+    tri_ref,
+    gate_hbm,
+    gate_ref,
     pair_ref,
-    row_valid_ref,
     col_valid_ref,
     in_gain_ref,
-    w_left_ref,
-    w_left_gate_ref,
-    w_right_ref,
-    w_right_gate_ref,
     w_out_gate_ref,
-    tri_ref,
-    gate_ref,
+    load_sem,
     normed,
     weights,
     staged,
@@ -61,10 +67,27 @@
     out_recv,
     local_sem,
 ):
-    rows = pair_ref.shape[0]
-    h_count = w_left_ref.shape[0]
+    rows = pair_hbm.shape[0]
+    h_count = w_left_hbm.shape[0]
     hc = h_count // chunks
     half = chips // 2
+    loads = [
+        pltpu.make_async_copy(source, target, load_sem.at[n])
+        for n, (source, target) in enumerate(
+            (
+                (pair_hbm, pair_ref),
+                (in_gain_hbm, in_gain_ref),
+                (col_valid_hbm, col_valid_ref),
+                (w_right_hbm, weights.at[0, :h_count]),
+                (w_right_gate_hbm, weights.at[0, h_count:]),
+                (w_left_hbm, weights.at[1, :h_count]),
+                (w_left_gate_hbm, weights.at[1, h_count:]),
+                (w_out_gate_hbm, w_out_gate_ref),
+            )
+        )
+    ]
+    for load in loads:
+        load.start()
     index = lax.axis_index("row")
     x = lax.axis_index("chan")
     core = lax.rem(index, 2)
@@ -95,10 +118,8 @@
     def at_heads(q):
         return pl.ds(q * hc, hc)
 
-    weights[0, :h_count] = w_right_ref[...]
-    weights[0, h_count:] = w_right_gate_ref[...]
-    weights[1, :h_count] = w_left_ref[...]
-    weights[1, h_count:] = w_left_gate_ref[...]
+    for load in loads:
+        load.wait()
     col_valid = col_valid_ref[...].astype(jnp.float32)
 
     def project(i, side, block):
@@ -202,12 +223,14 @@
             copy.start()
         own.start()
 
+    gate_copy = pltpu.make_async_copy(gate_ref, gate_hbm, load_sem.at[8])
     lax.fori_loop(0, rows, right_row, 0)
     quarter = rows // 4
     tasks = [functools.partial(turn_right, q) for q in range(2, chunks)]
     tasks += [functools.partial(lax.fori_loop, n * quarter, (n + 1) * quarter, left_row, 0) for n in range(4)]
     tasks += [send_left]
     tasks += [functools.partial(lax.fori_loop, n * quarter, (n + 1) * quarter, gate_row, 0) for n in range(4)]
+    tasks += [gate_copy.start]
 
     orders = ring_orders(chunks, half)
     steps = len(orders[0])
@@ -243,6 +266,7 @@
         for q, d in orders[way]:
             ring_copy(way, q, d).wait_send()
     left_copy.wait_send()
+    gate_copy.wait()
     for q in range(chunks):
         copies, own = out_copies(q)
         for copy in copies:
@@ -263,9 +287,15 @@
             jax.ShapeDtypeStruct((2 * h_count, rows, chips * 2 * rows), jnp.bfloat16),
             jax.ShapeDtypeStruct((rows, depth, w_out_gate.shape[1]), jnp.float32),
         ],
-        in_specs=[vmem, smem] + [vmem] * 7,
-        out_specs=[vmem, vmem],
+        in_specs=[smem] + [pl.BlockSpec(memory_space=pltpu.HBM)] * 8,
+        out_specs=[vmem, pl.BlockSpec(memory_space=pltpu.HBM)],
         scratch_shapes=[
+            pltpu.VMEM((rows, depth, w_out_gate.shape[1]), jnp.float32),
+            pltpu.VMEM((rows, depth, channels), jnp.bfloat16),
+            pltpu.VMEM((1, depth), jnp.int32),
+            pltpu.VMEM((1, channels), jnp.float32),
+            pltpu.VMEM(w_out_gate.shape, jnp.bfloat16),
+            dma((9,)),
             pltpu.VMEM((rows, depth, channels), jnp.bfloat16),
             pltpu.VMEM((2, 2 * h_count, channels), jnp.bfloat16),
             pltpu.VMEM((2, rows, h_count, depth), jnp.float32),
@@ -280,11 +310,11 @@
             dma((chunks,)),
         ],
         compiler_params=pltpu.CompilerParams(
-            collective_id=0, has_side_effects=True, vmem_limit_bytes=48 * 1024 * 1024
+            collective_id=0, has_side_effects=True, vmem_limit_bytes=60 * 1024 * 1024
         ),
     )(
+        residue_valid,
         pair_act,
-        residue_valid,
         residue_valid[None, :],
         in_gain[None, :],
         w_left.T,

time: 66 us -> 65.9 us (level)
  local copies, waits for them, and re-layouts: 6.47 us -> 1.59 us
  other arithmetic: 2.09 us -> 4.62 us
  Pallas kernels: 56.2 us -> 58.7 us
    unnamed x20 -> x8, local copies, waits for them, and re-layouts: 6.21 us -> 1.34 us
    pallas_call x1, Pallas kernels: 56.2 us -> 58.7 us  [triangle(): pl.pallas_call(functools.partial(triangle_kernel, chips, chunks), out_sha...]
    reduce_sum x1, other arithmetic: 0.2 us -> 1.51 us  [norm_axis(): mean = jnp.mean(values, axis=axis, keepdims=True)]
    reduce_sum x1, other arithmetic: 0.33 us -> 1.56 us  [norm_axis(): variance = jnp.mean(centered * centered, axis=axis, keepdims=True)]
where the time goes in v3:
time: 65.9 us; the launch traced here: 65.5 us
  Pallas kernels  58.7 us (89%)
  other arithmetic  4.62 us (7%)
  local copies, waits for them, and re-layouts  1.59 us (2%)
    pallas_call x1, Pallas kernels, triangle(): pl.pallas_call(functools.partial(triangle_kernel, chips, chunks), out_sha...  58.7 us
    reduce_sum x1, other arithmetic, norm_axis(): variance = jnp.mean(centered * centered, axis=axis, keepdims=True)  1.56 us
    reduce_sum x1, other arithmetic, norm_axis(): mean = jnp.mean(values, axis=axis, keepdims=True)  1.51 us
    unnamed x8, local copies, waits for them, and re-layouts  1.34 us

profile of v3, /device:TPU:0, one launch (start us, length us, event | category | flops | bytes accessed | tf_op | source)
XLA Modules:
  0.0 65.5 jit_solution(14867826176132212573)
XLA Ops:
  0.0 0.0 copy-start
  0.0 0.0 copy-start.3
  0.0 58.7 %shard_map.100 = (bf16[128,16,256]{2,1,0:T(8,128)(2,1)}, f32[16,256,128]{2,1,0:T(8,128)}) custom-call(s32[256]{0:T(256)} %row_valid_ref.1, bf16[16,256,128]{2,1,0:T(8,128)(2,1)} %pair_hbm.1, s32[1,256]{1,0:T(1,128)} %bitcast.21, f32[1,128]{1,0:T(1,128)} %bitcast.22, bf16[64,128]{1,0:T(8,128)(2,1)} %bitcast.17, bf16[64,128]{1,0:T(8,128)(2,1)} %bitcast.18, ...), custom_call_target="tpu_custom_call" | custom-call | tf_op jit(solution)/shard_map/pallas_call | solution.py:284
  58.7 0.0 copy-start.1
  58.7 1.5 %convert_reduce_fusion = f32[16,256]{1,0:T(8,128)S(1)} fusion(bf16[128,16,256]{2,1,0:T(8,128)(2,1)} %get-tuple-element.8), kind=kLoop, calls=%fused_computation.1 | loop fusion | flops 1044480 | bytes 1064960 | tf_op jit(solution)/shard_map/reduce_sum | solution.py:14
  60.2 1.6 %fusion.2 = f32[16,256]{1,0:T(8,128)S(1)} fusion(bf16[128,16,256]{2,1,0:T(8,128)(2,1)} %get-tuple-element.8, f32[16,256]{1,0:T(8,128)S(1)} %broadcast_multiply_fusion), kind=kLoop, calls=%fused_computation.4 | loop fusion | flops 2093056 | bytes 1081344 | tf_op jit(solution)/shard_map/reduce_sum | solution.py:16
  61.8 0.0 copy-done.3
  61.8 0.0 copy-done.1
  61.8 0.3 fusion.4
  62.2 0.0 copy-done
  62.2 0.6 fusion.6
  62.7 0.0 copy-start.2
  62.7 0.3 copy.12
  63.0 1.3 %copy-done.2 = f32[16,256,128]{2,1,0:T(8,128)S(1)} copy-done((f32[16,256,128]{2,1,0:T(8,128)S(1)}, f32[16,256,128]{2,1,0:T(8,128)}, u32[]{:S(2)}) %copy-start.2) | copy-done | bytes 2097176
  64.3 1.2 %fusion.5 = bf16[16,256,128]{2,1,0:T(8,128)(2,1)} fusion(f32[16,256,128]{2,1,0:T(8,128)S(1)} %copy-done.2, f32[16,2,8,16,128]{4,3,1,2,0:T(8,128)S(1)} %copy.12), kind=kLoop, calls=%fused_computation.8 | loop fusion | flops 1048576 | bytes 5242880 | tf_op jit(solution)/shard_map/convert_element_type | solution.py:339
  (2 shorter events, 0.0 us)
Async XLA Ops:
  0.0 62.2 %copy-start = (bf16[128,128]{1,0:T(8,128)(2,1)S(1)}, bf16[128,128]{1,0:T(8,128)(2,1)}, u32[]{:S(2)}) copy-start(bf16[128,128]{1,0:T(8,128)(2,1)} %param.18) | copy-start | bytes 98308
  0.0 61.8 %copy-start.3 = (f32[128]{0:T(128)S(1)}, f32[128]{0:T(128)}, u32[]{:S(2)}) copy-start(f32[128]{0:T(128)} %param.17) | copy-start | bytes 1540
  58.7 3.1 %copy-start.1 = (bf16[128,16,256]{2,1,0:T(8,128)(2,1)S(1)}, bf16[128,16,256]{2,1,0:T(8,128)(2,1)}, u32[]{:S(2)}) copy-start(bf16[128,16,256]{2,1,0:T(8,128)(2,1)} %get-tuple-element.8) | copy-start | bytes 3145732
  62.7 1.6 %copy-start.2 = (f32[16,256,128]{2,1,0:T(8,128)S(1)}, f32[16,256,128]{2,1,0:T(8,128)}, u32[]{:S(2)}) copy-start(f32[16,256,128]{2,1,0:T(8,128)} %get-tuple-element.7) | copy-start | bytes 6291460

commit v4 on v3

--- a/solution.py
+++ b/solution.py
@@ -7,6 +7,7 @@
 from jax.experimental.pallas import tpu as pltpu
 from jax.sharding import PartitionSpec as P
 
+CHUNKS = 4
 MESH = pl.DeviceIdType.MESH
 
 
@@ -46,9 +47,15 @@
     w_right_hbm,
     w_right_gate_hbm,
     w_out_gate_hbm,
+    out_gain_hbm,
+    w_out_hbm,
+    update_ref,
     tri_ref,
-    gate_hbm,
+    by_row,
     gate_ref,
+    out_gain_ref,
+    gain_columns,
+    w_out_ref,
     pair_ref,
     col_valid_ref,
     in_gain_ref,
@@ -83,6 +90,8 @@
                 (w_left_hbm, weights.at[1, :h_count]),
                 (w_left_gate_hbm, weights.at[1, h_count:]),
                 (w_out_gate_hbm, w_out_gate_ref),
+                (out_gain_hbm, out_gain_ref),
+                (w_out_hbm, w_out_ref),
             )
         )
     ]
@@ -201,6 +210,35 @@
         own = pltpu.make_async_copy(part.at[at_heads(q), at_rows(core)], target, local_sem.at[q])
         return copies, own
 
+    def collect(q):
+        copies, own = out_copies(q)
+        for copy in copies:
+            copy.wait_recv()
+        own.wait()
+        for side in range(2):
+            first = side * h_count + q * hc
+            by_row[:, first : first + hc, :] = jnp.swapaxes(
+                tri_ref[first : first + hc].astype(jnp.float32), 0, 1
+            )
+
+    def finish_row(i, carry):
+        values = by_row[i]
+        mean = jnp.mean(values, axis=0, keepdims=True)
+        centered = values - mean
+        variance = jnp.mean(centered * centered, axis=0, keepdims=True)
+        block = (centered * lax.rsqrt(variance + 1e-05) * gain_columns[:, :1]).astype(jnp.bfloat16)
+        projected = lax.dot_general(
+            block, w_out_ref[...], (((0,), (0,)), ((), ())), preferred_element_type=jnp.float32
+        )
+        for other in range(2):
+            for there in range(chips):
+                source = (other * chips + there) * rows
+                target = pl.ds((there * 2 + other) * rows, rows)
+                update_ref[i, target, :] = (
+                    gate_ref[i, target, :] * projected[source : source + rows]
+                ).astype(jnp.bfloat16)
+        return carry
+
     waited = set()
 
     def arrived(way, q, d):
@@ -223,14 +261,13 @@
             copy.start()
         own.start()
 
-    gate_copy = pltpu.make_async_copy(gate_ref, gate_hbm, load_sem.at[8])
-    lax.fori_loop(0, rows, right_row, 0)
+    lax.fori_loop(0, rows, right_row, 0, unroll=2)
+    gain_columns[...] = jnp.swapaxes(jnp.broadcast_to(out_gain_ref[...], gain_columns.shape), 0, 1)
     quarter = rows // 4
     tasks = [functools.partial(turn_right, q) for q in range(2, chunks)]
     tasks += [functools.partial(lax.fori_loop, n * quarter, (n + 1) * quarter, left_row, 0) for n in range(4)]
     tasks += [send_left]
     tasks += [functools.partial(lax.fori_loop, n * quarter, (n + 1) * quarter, gate_row, 0) for n in range(4)]
-    tasks += [gate_copy.start]
 
     orders = ring_orders(chunks, half)
     steps = len(orders[0])
@@ -254,6 +291,8 @@
             if done == 0:
                 left_copy.wait_recv()
             compute(done)
+            if done:
+                collect(done - 1)
             done += 1
     for task in tasks:
         task()
@@ -261,20 +300,21 @@
         left_copy.wait_recv()
     while done < chunks:
         compute(done)
+        if done:
+            collect(done - 1)
         done += 1
+    collect(chunks - 1)
+    lax.fori_loop(0, rows, finish_row, 0, unroll=2)
     for way in range(2):
         for q, d in orders[way]:
             ring_copy(way, q, d).wait_send()
     left_copy.wait_send()
-    gate_copy.wait()
     for q in range(chunks):
-        copies, own = out_copies(q)
-        for copy in copies:
-            copy.wait()
-        own.wait()
-
-
-def triangle(chips, chunks, pair_act, residue_valid, in_gain, w_left, w_left_gate, w_right, w_right_gate, w_out_gate):
+        for copy in out_copies(q)[0]:
+            copy.wait_send()
+
+
+def triangle(chips, chunks, pair_act, residue_valid, in_gain, w_left, w_left_gate, w_right, w_right_gate, out_gain, w_out, w_out_gate):
     rows, depth, channels = pair_act.shape
     h_count = w_left.shape[1]
     half = chips // 2
@@ -283,19 +323,21 @@
     smem = pl.BlockSpec(memory_space=pltpu.SMEM)
     return pl.pallas_call(
         functools.partial(triangle_kernel, chips, chunks),
-        out_shape=[
-            jax.ShapeDtypeStruct((2 * h_count, rows, chips * 2 * rows), jnp.bfloat16),
-            jax.ShapeDtypeStruct((rows, depth, w_out_gate.shape[1]), jnp.float32),
-        ],
-        in_specs=[smem] + [pl.BlockSpec(memory_space=pltpu.HBM)] * 8,
-        out_specs=[vmem, pl.BlockSpec(memory_space=pltpu.HBM)],
+        out_shape=jax.ShapeDtypeStruct((rows, depth, w_out.shape[1]), jnp.bfloat16),
+        in_specs=[smem] + [pl.BlockSpec(memory_space=pltpu.HBM)] * 10,
+        out_specs=vmem,
         scratch_shapes=[
+            pltpu.VMEM((2 * h_count, rows, chips * 2 * rows), jnp.bfloat16),
+            pltpu.VMEM((rows, 2 * h_count, chips * 2 * rows), jnp.float32),
             pltpu.VMEM((rows, depth, w_out_gate.shape[1]), jnp.float32),
+            pltpu.VMEM((1, 2 * h_count), jnp.float32),
+            pltpu.VMEM((2 * h_count, 2 * h_count), jnp.float32),
+            pltpu.VMEM(w_out.shape, jnp.bfloat16),
             pltpu.VMEM((rows, depth, channels), jnp.bfloat16),
             pltpu.VMEM((1, depth), jnp.int32),
             pltpu.VMEM((1, channels), jnp.float32),
             pltpu.VMEM(w_out_gate.shape, jnp.bfloat16),
-            dma((9,)),
+            dma((10,)),
             pltpu.VMEM((rows, depth, channels), jnp.bfloat16),
             pltpu.VMEM((2, 2 * h_count, channels), jnp.bfloat16),
             pltpu.VMEM((2, rows, h_count, depth), jnp.float32),
@@ -322,6 +364,8 @@
         w_right.T,
         w_right_gate.T,
         w_out_gate,
+        out_gain[None, :],
+        w_out,
     )
 
 
@@ -331,12 +375,7 @@
 
 
 def ring_body(chips, *operands):
-    out_gain, w_out, w_out_gate = operands[-3:]
-    tri_full, gate = triangle(chips, 4, *operands[:-3], w_out_gate)
-    projected = finish(tri_full, out_gain, w_out)
-    rows = operands[0].shape[0]
-    split = projected.reshape(rows, 2, chips, rows, projected.shape[-1])
-    return (gate * jnp.swapaxes(split, 1, 2).reshape(projected.shape)).astype(jnp.bfloat16)
+    return triangle(chips, CHUNKS, *operands)
 
 
 def body(*operands):

time: 65.9 us -> 62.5 us (0.948)
  other arithmetic: 4.62 us -> 0 us
  Pallas kernels: 58.7 us -> 59.5 us
  local copies, waits for them, and re-layouts: 1.59 us -> 2.3 us
    reduce_sum x2 -> x0, other arithmetic: 3.06 us -> none  [the longest x1 1.56 us: norm_axis(): variance = jnp.mean(centered * centered, axis=axis, keepdims=True)]
    convert_element_type x2 -> x0, other arithmetic: 1.54 us -> none  [the longest x1 1.21 us: ring_body(): (gate * jnp.swapaxes(split, 1, 2).reshape(projected.shape)).astype(jnp.bf...]
    unnamed x8 -> x1, local copies, waits for them, and re-layouts: 1.34 us -> 2.3 us
    pallas_call x1, Pallas kernels: 58.7 us -> 59.5 us  [triangle(): pl.pallas_call(functools.partial(triangle_kernel, chips, chunks), out_sha...]
where the time goes in v4:
time: 62.5 us; the launch traced here: 61.8 us
  Pallas kernels  59.5 us (95%)
  local copies, waits for them, and re-layouts  2.3 us (4%)
    pallas_call x1, Pallas kernels, triangle(): pl.pallas_call(functools.partial(triangle_kernel, chips, chunks), out_sha...  59.5 us
    unnamed x1, local copies, waits for them, and re-layouts  2.3 us

profile of v4, /device:TPU:0, one launch (start us, length us, event | category | flops | bytes accessed | tf_op | source)
XLA Modules:
  0.0 61.8 jit_solution(7019811666462096903)
XLA Ops:
  0.0 59.5 %shard_map.100 = bf16[16,256,128]{2,1,0:T(8,128)(2,1)} custom-call(s32[256]{0:T(256)} %row_valid_ref.1, bf16[16,256,128]{2,1,0:T(8,128)(2,1)} %pair_hbm.1, s32[1,256]{1,0:T(1,128)} %bitcast.11, f32[1,128]{1,0:T(1,128)} %bitcast.12, bf16[64,128]{1,0:T(8,128)(2,1)} %bitcast.7, bf16[64,128]{1,0:T(8,128)(2,1)} %bitcast.8, bf16[64,128]{1,0:T(8,128)(2,1)} %bitcast.9, ...), custom_call_target="tpu_custom_call" | custom-call | tf_op jit(solution)/shard_map/pallas_call | solution.py:324
  59.5 2.3 %copy.12 = bf16[16,256,128]{2,1,0:T(8,128)(2,1)} copy(bf16[16,256,128]{2,1,0:T(8,128)(2,1)} %shard_map.100) | data formatting | bytes 2097152

commit v5 on v4

--- a/solution.py
+++ b/solution.py
@@ -18,21 +18,17 @@
     return centered * lax.rsqrt(variance + 1e-05) * gain
 
 
-def ring_orders(chunks, half):
-    orders = []
-    for way in range(2):
-        order = []
-        for first in range(0, chunks, 2):
-            pair = [q for q in (first, first + 1) if q < chunks]
-            block = [(q, d) for d in range(1, half + 1) for q in pair]
-            block = [(q, d) for q, d in block if d < half or q % 2 == way]
-            if order:
-                tail = order.pop()
-                order += [block[0], tail] + block[1:]
-            else:
-                order = block
-        orders.append(order)
-    return orders
+def line_order(chunks, reach):
+    order = []
+    for first in range(0, chunks, 2):
+        pair = [q for q in (first, first + 1) if q < chunks]
+        block = [(q, d) for d in range(1, reach + 1) for q in pair]
+        if order:
+            tail = order.pop()
+            order += [block[0], tail] + block[1:]
+        else:
+            order = block
+    return order
 
 
 def triangle_kernel(
@@ -70,6 +66,8 @@
     sib_sem,
     ring_send,
     ring_recv,
+    pair_send,
+    pair_recv,
     out_send,
     out_recv,
     local_sem,
@@ -103,23 +101,24 @@
     chip = lax.div(index, 2)
     y = lax.rem(chip, 2)
     z = lax.div(chip, 2)
-    place = jnp.where(y == 0, z, chips - 1 - z)
-
-    def chip_at(ring_place):
-        spot = lax.rem(ring_place + 2 * chips, chips)
-        return jnp.where(spot < half, 2 * spot, 2 * (chips - 1 - spot) + 1)
-
+    reach = half - 1
     sibling = {"row": chip * 2 + (1 - core), "chan": x}
-    nexts = [
-        {"row": chip_at(place + 1) * 2 + core, "chan": x},
-        {"row": chip_at(place - 1) * 2 + core, "chan": x},
-    ]
+    nexts = [{"row": index + 4, "chan": x}, {"row": index - 4, "chan": x}]
+    has_next = [z < half - 1, z > 0]
+    beside = {"row": (2 * z + 1 - y) * 2 + core, "chan": x}
     across = {"row": index, "chan": 1 - x}
-    diagonal = {"row": chip * 2 + (1 - core), "chan": 1 - x}
+    diagonal = {"row": (2 * z + 1 - y) * 2 + core, "chan": 1 - x}
 
     barrier = pltpu.get_barrier_semaphore()
-    for partner in (sibling, nexts[0], nexts[1], across, diagonal):
+    for partner in (sibling, beside, across, diagonal):
         pl.semaphore_signal(barrier, inc=1, device_id=partner, device_id_type=MESH)
+    for way in range(2):
+
+        @pl.when(has_next[way])
+        def _():
+            pl.semaphore_signal(barrier, inc=1, device_id=nexts[way], device_id_type=MESH)
+
+    partners = 4 + jnp.where(z < half - 1, 1, 0) + jnp.where(z > 0, 1, 0)
 
     def at_rows(block):
         return pl.ds(pl.multiple_of(block * rows, rows), rows)
@@ -162,11 +161,17 @@
         return jnp.swapaxes(staged[side, :, q * hc : (q + 1) * hc, :], 0, 1).astype(jnp.bfloat16)
 
     def turn_right(q):
-        held[at_heads(q), at_rows(chip)] = turned(0, q)
+        held[at_heads(q), at_rows(2 * z + core)] = turned(0, q)
+
+
+    def origin(way, d):
+        return z - (1 - 2 * way) * d
+
+    def exists(way, d):
+        return origin(way, d) >= 0 if way == 0 else origin(way, d) < half
 
     def ring_copy(way, q, d):
-        step = 1 - 2 * way
-        spot = held.at[at_heads(q), at_rows(chip_at(place - step * (d - 1)))]
+        spot = held.at[at_heads(q), at_rows(2 * origin(way, d - 1) + core)]
         return pltpu.make_async_remote_copy(
             src_ref=spot,
             dst_ref=spot,
@@ -176,27 +181,47 @@
             device_id_type=MESH,
         )
 
-    left_spot = lefts.at[:, at_rows(core)]
+    def sibling_copy(way, q, d):
+        spot = held.at[at_heads(q), at_rows(2 * origin(way, d) + core)]
+        return pltpu.make_async_remote_copy(
+            src_ref=spot,
+            dst_ref=spot,
+            send_sem=pair_send.at[way, q, d],
+            recv_sem=pair_recv.at[way, q, d],
+            device_id=sibling,
+            device_id_type=MESH,
+        )
+
+    def each_piece(q, act):
+        act(sibling_copy(0, q, 0))
+        for way in range(2):
+            for d in range(1, reach + 1):
+
+                @pl.when(exists(way, d))
+                def _():
+                    act(sibling_copy(way, q, d))
+
+    left_spot = lefts.at[:, at_rows(y)]
     left_copy = pltpu.make_async_remote_copy(
         src_ref=left_spot,
         dst_ref=left_spot,
         send_sem=sib_sem.at[0],
         recv_sem=sib_sem.at[1],
-        device_id=sibling,
+        device_id=beside,
         device_id_type=MESH,
     )
 
     def send_left():
         for q in range(chunks):
-            lefts[at_heads(q), at_rows(core)] = turned(1, q)
+            lefts[at_heads(q), at_rows(y)] = turned(1, q)
         left_copy.start()
 
     def out_copies(q):
         target = tri_ref.at[
-            pl.ds(x * h_count + q * hc, hc), :, pl.ds(pl.multiple_of(core * rows * chips, 128), rows * chips)
+            pl.ds(x * h_count + q * hc, hc), :, pl.ds(pl.multiple_of(y * rows * chips, 128), rows * chips)
         ]
         copies = []
-        for n, (device, owner) in enumerate(((across, core), (diagonal, 1 - core), (sibling, 1 - core))):
+        for n, (device, owner) in enumerate(((across, y), (diagonal, 1 - y), (beside, 1 - y))):
             copies.append(
                 pltpu.make_async_remote_copy(
                     src_ref=part.at[at_heads(q), at_rows(owner)],
@@ -207,7 +232,7 @@
                     device_id_type=MESH,
                 )
             )
-        own = pltpu.make_async_copy(part.at[at_heads(q), at_rows(core)], target, local_sem.at[q])
+        own = pltpu.make_async_copy(part.at[at_heads(q), at_rows(y)], target, local_sem.at[q])
         return copies, own
 
     def collect(q):
@@ -231,11 +256,11 @@
             block, w_out_ref[...], (((0,), (0,)), ((), ())), preferred_element_type=jnp.float32
         )
         for other in range(2):
-            for there in range(chips):
-                source = (other * chips + there) * rows
-                target = pl.ds((there * 2 + other) * rows, rows)
+            for there in range(half):
+                source = (other * half + there) * 2 * rows
+                target = pl.ds((there * 2 + other) * 2 * rows, 2 * rows)
                 update_ref[i, target, :] = (
-                    gate_ref[i, target, :] * projected[source : source + rows]
+                    gate_ref[i, target, :] * projected[source : source + 2 * rows]
                 ).astype(jnp.bfloat16)
         return carry
 
@@ -243,14 +268,18 @@
 
     def arrived(way, q, d):
         if (way, q, d) not in waited:
-            ring_copy(way, q, d).wait_recv()
             waited.add((way, q, d))
 
+            @pl.when(exists(way, d))
+            def _():
+                ring_copy(way, q, d).wait_recv()
+                sibling_copy(way, q, d).start()
+
     def compute(q):
-        for way in range(2):
-            top = half if q % 2 == way else half - 1
-            for d in range(1, top + 1):
+        for d in range(1, reach + 1):
+            for way in range(2):
                 arrived(way, q, d)
+        each_piece(q, lambda copy: copy.wait_recv())
         heads = at_heads(q)
         product = lax.dot_general(
             lefts[heads], held[heads], (((2,), (2,)), ((0,), (0,))), preferred_element_type=jnp.float32
@@ -269,24 +298,30 @@
     tasks += [send_left]
     tasks += [functools.partial(lax.fori_loop, n * quarter, (n + 1) * quarter, gate_row, 0) for n in range(4)]
 
-    orders = ring_orders(chunks, half)
-    steps = len(orders[0])
+    order = line_order(chunks, reach)
+    steps = len(order)
     done = 0
     for n in range(steps):
         if n < 2:
             turn_right(n)
         if n == 0:
-            pl.semaphore_wait(barrier, 5)
+            pl.semaphore_wait(barrier, partners)
+        q, d = order[n]
         for way in range(2):
-            q, d = orders[way][n]
             if d > 1:
                 arrived(way, q, d - 1)
-            ring_copy(way, q, d).start()
+
+            @pl.when(has_next[way] & exists(way, d - 1) if d > 1 else has_next[way])
+            def _():
+                ring_copy(way, q, d).start()
+
+        if d == 1:
+            sibling_copy(0, q, 0).start()
         if n >= 1:
             for task in tasks[:2]:
                 task()
             tasks = tasks[2:]
-        last = max(orders[w].index((done, half if done % 2 == w else half - 1)) for w in range(2))
+        last = order.index((done, reach))
         if n >= last + 2 and n < steps - 1 and not tasks:
             if done == 0:
                 left_copy.wait_recv()
@@ -305,9 +340,15 @@
         done += 1
     collect(chunks - 1)
     lax.fori_loop(0, rows, finish_row, 0, unroll=2)
-    for way in range(2):
-        for q, d in orders[way]:
-            ring_copy(way, q, d).wait_send()
+    for q, d in order:
+        for way in range(2):
+
+            @pl.when(has_next[way] & exists(way, d - 1) if d > 1 else has_next[way])
+            def _():
+                ring_copy(way, q, d).wait_send()
+
+    for q in range(chunks):
+        each_piece(q, lambda copy: copy.wait_send())
     left_copy.wait_send()
     for q in range(chunks):
         for copy in out_copies(q)[0]:
@@ -347,6 +388,8 @@
             dma((2,)),
             dma((2, chunks, half)),
             dma((2, chunks, half)),
+            dma((2, chunks, half)),
+            dma((2, chunks, half)),
             dma((3, chunks)),
             dma((3, chunks)),
             dma((chunks,)),

time: 62.5 us -> 61.1 us (0.978)
  Pallas kernels: 59.5 us -> 58.6 us
    pallas_call x1, Pallas kernels: 59.5 us -> 58.6 us  [triangle(): pl.pallas_call(functools.partial(triangle_kernel, chips, chunks), out_sha...]
where the time goes in v5:
time: 61.1 us; the launch traced here: 60.9 us
  Pallas kernels  58.6 us (96%)
  local copies, waits for them, and re-layouts  2.3 us (4%)
    pallas_call x1, Pallas kernels, triangle(): pl.pallas_call(functools.partial(triangle_kernel, chips, chunks), out_sha...  58.6 us
    unnamed x1, local copies, waits for them, and re-layouts  2.3 us

profile of v5, /device:TPU:0, one launch (start us, length us, event | category | flops | bytes accessed | tf_op | source)
XLA Modules:
  0.0 60.9 jit_solution(2658481144175265267)
XLA Ops:
  0.0 58.6 %shard_map.100 = bf16[16,256,128]{2,1,0:T(8,128)(2,1)} custom-call(s32[256]{0:T(256)} %row_valid_ref.1, bf16[16,256,128]{2,1,0:T(8,128)(2,1)} %pair_hbm.1, s32[1,256]{1,0:T(1,128)} %bitcast.11, f32[1,128]{1,0:T(1,128)} %bitcast.12, bf16[64,128]{1,0:T(8,128)(2,1)} %bitcast.7, bf16[64,128]{1,0:T(8,128)(2,1)} %bitcast.8, bf16[64,128]{1,0:T(8,128)(2,1)} %bitcast.9, ...), custom_call_target="tpu_custom_call" | custom-call | tf_op jit(solution)/shard_map/pallas_call | solution.py:365
  58.6 2.3 %copy.12 = bf16[16,256,128]{2,1,0:T(8,128)(2,1)} copy(bf16[16,256,128]{2,1,0:T(8,128)(2,1)} %shard_map.100) | data formatting | bytes 2097152

commit v6 on v5

--- a/solution.py
+++ b/solution.py
@@ -7,7 +7,8 @@
 from jax.experimental.pallas import tpu as pltpu
 from jax.sharding import PartitionSpec as P
 
-CHUNKS = 4
+CHUNKS = 8
+GROUP = 4
 MESH = pl.DeviceIdType.MESH
 
 
@@ -20,8 +21,8 @@
 
 def line_order(chunks, reach):
     order = []
-    for first in range(0, chunks, 2):
-        pair = [q for q in (first, first + 1) if q < chunks]
+    for first in range(0, chunks, GROUP):
+        pair = range(first, min(first + GROUP, chunks))
         block = [(q, d) for d in range(1, reach + 1) for q in pair]
         if order:
             tail = order.pop()
@@ -293,7 +294,7 @@
     lax.fori_loop(0, rows, right_row, 0, unroll=2)
     gain_columns[...] = jnp.swapaxes(jnp.broadcast_to(out_gain_ref[...], gain_columns.shape), 0, 1)
     quarter = rows // 4
-    tasks = [functools.partial(turn_right, q) for q in range(2, chunks)]
+    tasks = [functools.partial(turn_right, q) for q in range(GROUP, chunks)]
     tasks += [functools.partial(lax.fori_loop, n * quarter, (n + 1) * quarter, left_row, 0) for n in range(4)]
     tasks += [send_left]
     tasks += [functools.partial(lax.fori_loop, n * quarter, (n + 1) * quarter, gate_row, 0) for n in range(4)]
@@ -302,7 +303,7 @@
     steps = len(order)
     done = 0
     for n in range(steps):
-        if n < 2:
+        if n < GROUP:
             turn_right(n)
         if n == 0:
             pl.semaphore_wait(barrier, partners)
@@ -318,9 +319,9 @@
         if d == 1:
             sibling_copy(0, q, 0).start()
         if n >= 1:
-            for task in tasks[:2]:
+            for task in tasks[:1]:
                 task()
-            tasks = tasks[2:]
+            tasks = tasks[1:]
         last = order.index((done, reach))
         if n >= last + 2 and n < steps - 1 and not tasks:
             if done == 0:

time: 61.1 us -> 67.2 us (1.100)
  Pallas kernels: 58.6 us -> 64.7 us
    pallas_call x1, Pallas kernels: 58.6 us -> 64.7 us  [triangle(): pl.pallas_call(functools.partial(triangle_kernel, chips, chunks), out_sha...]
where the time goes in v6:
time: 67.2 us; the launch traced here: 67 us
  Pallas kernels  64.7 us (96%)
  local copies, waits for them, and re-layouts  2.3 us (3%)
    pallas_call x1, Pallas kernels, triangle(): pl.pallas_call(functools.partial(triangle_kernel, chips, chunks), out_sha...  64.7 us
    unnamed x1, local copies, waits for them, and re-layouts  2.3 us

profile of v6, /device:TPU:0, one launch (start us, length us, event | category | flops | bytes accessed | tf_op | source)
XLA Modules:
  0.0 67.0 jit_solution(18364982027076019204)
XLA Ops:
  0.0 64.7 %shard_map.100 = bf16[16,256,128]{2,1,0:T(8,128)(2,1)} custom-call(s32[256]{0:T(256)} %row_valid_ref.1, bf16[16,256,128]{2,1,0:T(8,128)(2,1)} %pair_hbm.1, s32[1,256]{1,0:T(1,128)} %bitcast.11, f32[1,128]{1,0:T(1,128)} %bitcast.12, bf16[64,128]{1,0:T(8,128)(2,1)} %bitcast.7, bf16[64,128]{1,0:T(8,128)(2,1)} %bitcast.8, bf16[64,128]{1,0:T(8,128)(2,1)} %bitcast.9, ...), custom_call_target="tpu_custom_call" | custom-call | tf_op jit(solution)/shard_map/pallas_call | solution.py:366
  64.7 2.3 %copy.12 = bf16[16,256,128]{2,1,0:T(8,128)(2,1)} copy(bf16[16,256,128]{2,1,0:T(8,128)(2,1)} %shard_map.100) | data formatting | bytes 2097152
